TPU v7x, 512 devices: a whole 4x8x8 slice. The times are simulated.
512 devices in a mesh: member: 8 (over x, z_hi), node: 64 (over z_lo, y, core).
Axes of the slice: x: 4, y: 8, z: 8 (z_hi: 2, z_lo: 4; z = z_hi * 4 + z_lo), core: 2. Of those that a mesh axis runs over, the one named last changes fastest.
Arguments:
- latent: bfloat16 [16, 16384, 512], P('member', 'node'), may hold values from -6 to 6
- noise_draw: float32 [16, 32], P('member'), may hold values from -4 to 4
- mesh_links: int32 [6, 16384], P(None, 'node'), may hold values from 0 to 16383, as said below
- w_cond: float32 [2, 32, 512], replicated, may hold values from -0.3 to 0.3
- w_in: bfloat16 [2, 1024, 512], replicated, may hold values from -0.1875 to 0.1875
- w_out: bfloat16 [2, 512, 512], replicated, may hold values from -0.25 to 0.25
- dec_gain: float32 [512], replicated, may hold values from 0.5 to 1.5
- w_dec: bfloat16 [83, 512], replicated, may hold values from -2 to 2
- target_vertex_map: int32 [65536], P('node'), may hold values from 0 to 16383, as said below
- prior_field: bfloat16 [83, 65536], P(None, 'node'), may hold values from -6 to 6
- target: bfloat16 [83, 65536], P(None, 'node'), may hold values from -6 to 6
- location_loss_factor: float32 [65536], P('node'), may hold values from 8 to 24
Outputs:
- prediction_sensitivity: bfloat16 [16, 83, 65536], P('member', None, 'node')
- vertex_attribute_sensitivity: bfloat16 [16, 16384, 512], P('member', 'node')
Inputs may be any that keep to these rules, and one draw needn't show every extreme that they name: mesh_links[k, n] = (n + s) mod 16384 with 1 <= |s| <= 96: every neighbour of a node lies within 96 positions of it along the node order, counted around the end. target_vertex_map[g] // 256 == g // 1024.
All inputs are finite; a program needn't handle non-finite values.
Results may differ from a plain program's by a relative error of at most 0.007.
Values may be sent and summed in bfloat16 or wider, within the bound.
No kernel may reach another device: no remote copies, remote signals or barrier semaphores. Data moves between devices by JAX's collectives and lax.ppermute only.
A program may use at most 64 MiB of HBM per device.

v0:
```python
import jax
import jax.numpy as jnp
from jax import lax
from jax.sharding import PartitionSpec as P

WIN = 96


NORM_EPS = 1e-06
DIST_EPS = 1e-06


def extended(cells, sides, width):
    for axis, dim in sides:
        count = lax.axis_size(axis)
        head = lax.slice_in_dim(cells, 0, width, axis=dim)
        tail = lax.slice_in_dim(cells, cells.shape[dim] - width, cells.shape[dim], axis=dim)
        cells = jnp.concatenate(
            [
                lax.ppermute(tail, axis, [(i, (i + 1) % count) for i in range(count)]),
                cells,
                lax.ppermute(head, axis, [((i + 1) % count, i) for i in range(count)]),
            ],
            axis=dim,
        )
    return cells


def apply_layer_norm(values, scaling):
    inverse = lax.rsqrt(jnp.mean(values * values, axis=-1, keepdims=True) + NORM_EPS)
    return (values * inverse * scaling).astype(jnp.bfloat16)


def neighbour_mean(normalized_rows, mesh_links, first_row, node_total, margin):
    inner_rows = mesh_links.shape[1]
    positions = jnp.arange(inner_rows, dtype=jnp.int32)
    own_global = first_row + margin + positions
    summed = jnp.zeros(
        (normalized_rows.shape[0], inner_rows, normalized_rows.shape[2]), jnp.float32
    )
    for slot_index in range(mesh_links.shape[0]):
        offsets = jnp.mod(mesh_links[slot_index] - own_global + margin, node_total) - margin
        summed = summed + jnp.take(normalized_rows, margin + positions + offsets, axis=1).astype(
            jnp.float32
        )
    return (summed / mesh_links.shape[0]).astype(jnp.bfloat16)


def layer_update(normed_rows, neighbours, w_in_layer, w_out_layer):
    joined = jnp.concatenate([normed_rows, neighbours], axis=2)
    preact = jnp.einsum("mrk,kl->mrl", joined, w_in_layer, preferred_element_type=jnp.float32)
    activated = jax.nn.silu(preact).astype(jnp.bfloat16)
    return jnp.einsum("mrk,kl->mrl", activated, w_out_layer, preferred_element_type=jnp.float32)


def pull_total(anchors, others, initial):

    def add_pull(carried, other_member):
        offset = anchors - other_member.astype(jnp.float32)[None]
        spread = jnp.sqrt(jnp.sum(offset * offset, axis=1, keepdims=True) + DIST_EPS)
        return (carried + offset / spread, None)

    return lax.scan(add_pull, initial, others)[0]


def score_grad(anchors, pull_sums, truth_rows, weights, ensemble):
    missed = anchors - truth_rows.astype(jnp.float32)[None]
    reached = jnp.sqrt(jnp.sum(missed * missed, axis=1, keepdims=True) + DIST_EPS)
    skill_measures = missed / (ensemble * reached) - pull_sums / (ensemble * (ensemble - 1))
    return (weights[None, None, :] * skill_measures).astype(jnp.bfloat16)


def per_device(
    latent,
    noise_draw,
    mesh_links,
    w_cond,
    w_in,
    w_out,
    dec_gain,
    w_dec,
    target_vertex_map,
    prior_field,
    target,
    location_loss_factor,
):
    local_ensemble_slice = latent.shape[0]
    node_rows = latent.shape[1]
    node_total = node_rows * lax.axis_size("node")
    first_node = lax.axis_index("node") * node_rows
    reach_rows = WIN
    layer_count = w_in.shape[0]
    noise_scale_factors = [
        (1.0 + jnp.dot(noise_draw, w_cond[current_layer_index], precision=lax.Precision.HIGHEST))[
            :, None, :
        ]
        for current_layer_index in range(layer_count)
    ]
    processor_state = latent.astype(jnp.float32)
    for current_layer_index in range(layer_count):
        normalized_rows = apply_layer_norm(
            processor_state, noise_scale_factors[current_layer_index]
        )
        widened = extended(normalized_rows, (("node", 1),), reach_rows)
        neighbours = neighbour_mean(
            widened, mesh_links, first_node - reach_rows, node_total, reach_rows
        )
        processor_state = processor_state + layer_update(
            normalized_rows, neighbours, w_in[current_layer_index], w_out[current_layer_index]
        )
    features = apply_layer_norm(processor_state, dec_gain)
    readout_result = jnp.einsum("cl,mnl->mcn", w_dec, features, preferred_element_type=jnp.float32)
    local_assign = target_vertex_map - first_node
    ensemble_prediction = (
        prior_field.astype(jnp.float32)[None] + jnp.take(readout_result, local_assign, axis=2)
    ).astype(jnp.bfloat16)
    variable_total = ensemble_prediction.shape[1]
    location_entries = ensemble_prediction.shape[2]
    member_group_lists = lax.axis_size("member")
    ensemble = local_ensemble_slice * member_group_lists
    section_rows = location_entries // member_group_lists
    partition_pieces = ensemble_prediction.reshape(
        local_ensemble_slice, variable_total, member_group_lists, section_rows
    )
    regrouped = lax.all_to_all(
        partition_pieces, "member", split_axis=2, concat_axis=0, tiled=True
    ).reshape(ensemble, variable_total, section_rows)
    piece_start = lax.axis_index("member") * section_rows
    anchors = regrouped.astype(jnp.float32)
    pull_sums = pull_total(anchors, regrouped, jnp.zeros_like(anchors))
    truth_rows = lax.dynamic_slice_in_dim(target, piece_start, section_rows, 1)
    weights = lax.dynamic_slice_in_dim(location_loss_factor, piece_start, section_rows, 0)
    patch_grad = score_grad(anchors, pull_sums, truth_rows, weights, ensemble)
    yielded_results = lax.all_to_all(
        patch_grad.reshape(ensemble, variable_total, 1, section_rows),
        "member",
        split_axis=0,
        concat_axis=2,
        tiled=True,
    )
    prediction_sensitivity = yielded_results.reshape(
        local_ensemble_slice, variable_total, location_entries
    )
    node_ids = jnp.arange(node_rows, dtype=jnp.int32)
    incidence = (local_assign[:, None] == node_ids[None, :]).astype(jnp.bfloat16)
    vertex_sensitivity = jnp.dot(
        prediction_sensitivity.reshape(local_ensemble_slice * variable_total, location_entries),
        incidence,
        preferred_element_type=jnp.float32,
    ).reshape(local_ensemble_slice, variable_total, node_rows)
    vertex_attribute_sensitivity = jnp.einsum(
        "mcn,cl->mnl",
        vertex_sensitivity,
        w_dec.astype(jnp.float32),
        precision=lax.Precision.HIGHEST,
    ).astype(jnp.bfloat16)
    return (prediction_sensitivity, vertex_attribute_sensitivity)


def solution(mesh):
    in_specs = (
        P("member", "node", None),
        P("member", None),
        P(None, "node"),
        P(),
        P(),
        P(),
        P(),
        P(),
        P("node"),
        P(None, "node"),
        P(None, "node"),
        P("node"),
    )
    out_specs = (P("member", None, "node"), P("member", "node", None))
    return jax.shard_map(
        per_device, mesh=mesh, in_specs=in_specs, out_specs=out_specs, check_vma=False
    )
```

profile of v0, /device:TPU:2, one launch (start us, length us, event | category | flops | bytes accessed | tf_op | source)
XLA Modules:
  0.0 127.1 jit_solution(6112845105319158139)
XLA Ops:
  0.7 1.3 %fusion = f32[2,256]{1,0:T(2,128)S(1)} fusion(bf16[2,256,512]{2,1,0:T(8,128)(2,1)} %param.16), kind=kLoop, calls=%fused_computation.25 | loop fusion | flops 785920 | bytes 526336 | tf_op jit(solution)/shard_map/reduce_sum | solution.py:30
  2.0 1.0 convolution_add_fusion.2
  3.0 1.2 fusion.2
  4.3 1.9 %collective-permute-start = (bf16[2,96,512]{2,1,0:T(8,128)(2,1)S(1)}, bf16[2,96,512]{2,1,0:T(8,128)(2,1)S(1)}, u32[]{:S(2)}, u32[]{:S(2)}) collective-permute-start(bf16[2,96,512]{2,1,0:T(8,128)(2,1)S(1)} %get-tuple-element.87), channel_id=1, source_target_pairs={{0,1},{1,2},{2,3},{3,4},{4,5},{5,6},{6,7},{7,8},{8,9},{9,10},{10,1... | collective-permute-start | bytes 589832 | tf_op jit(solution)/shard_map/ppermute | solution.py:20
  6.2 10.2 %collective-permute-start.1 = (bf16[2,96,512]{2,1,0:T(8,128)(2,1)S(1)}, bf16[2,96,512]{2,1,0:T(8,128)(2,1)S(1)}, u32[]{:S(2)}, u32[]{:S(2)}) collective-permute-start(bf16[2,96,512]{2,1,0:T(8,128)(2,1)S(1)} %get-tuple-element.88), channel_id=1, source_target_pairs={{1,0},{2,1},{3,2},{4,3},{5,4},{6,5},{7,6},{8,7},{9,8},{10,9},{11,1... | collective-permute-start | bytes 589832 | tf_op jit(solution)/shard_map/ppermute | solution.py:22
  17.9 1.8 %collective-permute-done.1 = bf16[2,96,512]{2,1,0:T(8,128)(2,1)S(1)} collective-permute-done((bf16[2,96,512]{2,1,0:T(8,128)(2,1)S(1)}, bf16[2,96,512]{2,1,0:T(8,128)(2,1)S(1)}, u32[]{:S(2)}, u32[]{:S(2)}) %collective-permute-start.1) | collective-permute-done | bytes 196640 | tf_op jit(solution)/shard_map/ppermute | solution.py:22
  20.7 1.7 %gather_fusion.1 = bf16[256,2,512]{2,1,0:T(2,128)(2,1)S(1)} fusion(bf16[2,448,512]{2,0,1:T(2,128)(2,1)S(1)} %copy.178, s32[1024]{0:T(1024)S(1)} %pad_clamp_fusion.5), kind=kCustom, calls=%fused_computation.clone | custom fusion | bytes 1049600 | tf_op jit(solution)/shard_map/jit(_take)/gather | solution.py:43
  22.4 1.7 %gather_fusion.2 = bf16[256,2,512]{2,1,0:T(2,128)(2,1)S(1)} fusion(bf16[2,448,512]{2,0,1:T(2,128)(2,1)S(1)} %copy.178, s32[1024]{0:T(1024)S(1)} %pad_clamp_fusion.4), kind=kCustom, calls=%fused_computation.1.clone | custom fusion | bytes 1049600 | tf_op jit(solution)/shard_map/jit(_take)/gather | solution.py:43
  24.2 1.7 %gather_fusion.3 = bf16[256,2,512]{2,1,0:T(2,128)(2,1)S(1)} fusion(bf16[2,448,512]{2,0,1:T(2,128)(2,1)S(1)} %copy.178, s32[1024]{0:T(1024)S(1)} %pad_clamp_fusion.3), kind=kCustom, calls=%fused_computation.2.clone | custom fusion | bytes 1049600 | tf_op jit(solution)/shard_map/jit(_take)/gather | solution.py:43
  25.9 2.5 %gather_fusion.4 = bf16[256,2,512]{2,1,0:T(2,128)(2,1)} fusion(bf16[2,448,512]{2,0,1:T(2,128)(2,1)S(1)} %copy.178, s32[1024]{0:T(1024)S(1)} %pad_clamp_fusion.2), kind=kCustom, calls=%fused_computation.3.clone | custom fusion | bytes 1049600 | tf_op jit(solution)/shard_map/jit(_take)/gather | solution.py:43
  28.4 2.5 %gather_fusion.5 = bf16[256,2,512]{2,1,0:T(2,128)(2,1)} fusion(bf16[2,448,512]{2,0,1:T(2,128)(2,1)S(1)} %copy.178, s32[1024]{0:T(1024)S(1)} %pad_clamp_fusion.1), kind=kCustom, calls=%fused_computation.4.clone | custom fusion | bytes 1049600 | tf_op jit(solution)/shard_map/jit(_take)/gather | solution.py:43
  30.9 2.5 %gather_fusion.6 = bf16[256,2,512]{2,1,0:T(2,128)(2,1)} fusion(bf16[2,448,512]{2,0,1:T(2,128)(2,1)S(1)} %copy.178, s32[1024]{0:T(1024)S(1)} %pad_clamp_fusion), kind=kCustom, calls=%fused_computation.5.clone | custom fusion | bytes 1049600 | tf_op jit(solution)/shard_map/jit(_take)/gather | solution.py:43
  33.4 2.8 %multiply_convert_fusion.5 = bf16[2,256,512]{2,1,0:T(8,128)(2,1)} fusion(bf16[256,2,512]{2,1,0:T(2,128)(2,1)} %gather_fusion.6, bf16[256,2,512]{2,1,0:T(2,128)(2,1)} %gather_fusion.5, bf16[256,2,512]{2,1,0:T(2,128)(2,1)} %gather_fusion.4, bf16[256,2,512]{2,1,0:T(2,128)(2,1)S(1)} %gather_fusion.3, bf16[256,2,512]{2,1,0:T(2,128)(2,1)S(1)} %gather_fusion.2, ...), kind=kLoop, calls=%fused_computation.48 | loop fusion | flops 4980736 | bytes 3671552 | tf_op jit(solution)/shard_map/convert_element_type | solution.py:46
  36.2 2.7 %multiply_reduce_fusion.2 = (f32[2,256]{1,0:T(2,128)S(1)}, f32[2,256,512]{2,1,0:T(8,128)S(1)}) fusion(bf16[2,512,512]{2,1,0:T(8,128)(2,1)} %param.21, bf16[2,1024,512]{2,1,0:T(8,128)(2,1)} %param.20, bf16[2,256,512]{2,1,0:T(8,128)(2,1)} %multiply_convert_fusion.5, bf16[2,256,512]{2,1,0:T(8,128)(2,1)S(1)} %fusion.2, bf16[2,256,512]{2,1,0:T(8,128)(2,1)S(1)} %copy-done.1), kind=kOutput, calls=%fused_computation.45 | convolution fusion | flops 809762304 | bytes 4196352 | tf_op jit(solution)/shard_map/mrk,kl->mrl/dot_general | solution.py:53
  39.1 1.9 %collective-permute-start.2 = (bf16[2,96,512]{2,1,0:T(8,128)(2,1)S(1)}, bf16[2,96,512]{2,1,0:T(8,128)(2,1)S(1)}, u32[]{:S(2)}, u32[]{:S(2)}) collective-permute-start(bf16[2,96,512]{2,1,0:T(8,128)(2,1)S(1)} %get-tuple-element.85), channel_id=1, source_target_pairs={{0,1},{1,2},{2,3},{3,4},{4,5},{5,6},{6,7},{7,8},{8,9},{9,10},{10,1... | collective-permute-start | bytes 589832 | tf_op jit(solution)/shard_map/ppermute | solution.py:20
  41.1 7.9 %collective-permute-start.3 = (bf16[2,96,512]{2,1,0:T(8,128)(2,1)S(1)}, bf16[2,96,512]{2,1,0:T(8,128)(2,1)S(1)}, u32[]{:S(2)}, u32[]{:S(2)}) collective-permute-start(bf16[2,96,512]{2,1,0:T(8,128)(2,1)S(1)} %get-tuple-element.86), channel_id=1, source_target_pairs={{1,0},{2,1},{3,2},{4,3},{5,4},{6,5},{7,6},{8,7},{9,8},{10,9},{11,1... | collective-permute-start | bytes 589832 | tf_op jit(solution)/shard_map/ppermute | solution.py:22
  49.0 1.2 collective-permute-done.2
  50.2 1.8 %collective-permute-done.3 = bf16[2,96,512]{2,1,0:T(8,128)(2,1)S(1)} collective-permute-done((bf16[2,96,512]{2,1,0:T(8,128)(2,1)S(1)}, bf16[2,96,512]{2,1,0:T(8,128)(2,1)S(1)}, u32[]{:S(2)}, u32[]{:S(2)}) %collective-permute-start.3) | collective-permute-done | bytes 196640 | tf_op jit(solution)/shard_map/ppermute | solution.py:22
  53.0 1.7 %gather_fusion.7 = bf16[256,2,512]{2,1,0:T(2,128)(2,1)S(1)} fusion(bf16[2,448,512]{2,0,1:T(2,128)(2,1)S(1)} %copy.190, s32[1024]{0:T(1024)S(1)} %pad_clamp_fusion.5), kind=kCustom, calls=%fused_computation.6.clone | custom fusion | bytes 1049600 | tf_op jit(solution)/shard_map/jit(_take)/gather | solution.py:43
  54.7 1.7 %gather_fusion.8 = bf16[256,2,512]{2,1,0:T(2,128)(2,1)S(1)} fusion(bf16[2,448,512]{2,0,1:T(2,128)(2,1)S(1)} %copy.190, s32[1024]{0:T(1024)S(1)} %pad_clamp_fusion.4), kind=kCustom, calls=%fused_computation.7.clone | custom fusion | bytes 1049600 | tf_op jit(solution)/shard_map/jit(_take)/gather | solution.py:43
  56.5 1.7 %gather_fusion.9 = bf16[256,2,512]{2,1,0:T(2,128)(2,1)S(1)} fusion(bf16[2,448,512]{2,0,1:T(2,128)(2,1)S(1)} %copy.190, s32[1024]{0:T(1024)S(1)} %pad_clamp_fusion.3), kind=kCustom, calls=%fused_computation.8.clone | custom fusion | bytes 1049600 | tf_op jit(solution)/shard_map/jit(_take)/gather | solution.py:43
  58.2 2.5 %gather_fusion.10 = bf16[256,2,512]{2,1,0:T(2,128)(2,1)} fusion(bf16[2,448,512]{2,0,1:T(2,128)(2,1)S(1)} %copy.190, s32[1024]{0:T(1024)S(1)} %pad_clamp_fusion.2), kind=kCustom, calls=%fused_computation.9.clone | custom fusion | bytes 1049600 | tf_op jit(solution)/shard_map/jit(_take)/gather | solution.py:43
  60.7 2.5 %gather_fusion.11 = bf16[256,2,512]{2,1,0:T(2,128)(2,1)} fusion(bf16[2,448,512]{2,0,1:T(2,128)(2,1)S(1)} %copy.190, s32[1024]{0:T(1024)S(1)} %pad_clamp_fusion.1), kind=kCustom, calls=%fused_computation.10.clone | custom fusion | bytes 1049600 | tf_op jit(solution)/shard_map/jit(_take)/gather | solution.py:43
  63.2 2.5 %gather_fusion.12 = bf16[256,2,512]{2,1,0:T(2,128)(2,1)} fusion(bf16[2,448,512]{2,0,1:T(2,128)(2,1)S(1)} %copy.190, s32[1024]{0:T(1024)S(1)} %pad_clamp_fusion), kind=kCustom, calls=%fused_computation.11.clone | custom fusion | bytes 1049600 | tf_op jit(solution)/shard_map/jit(_take)/gather | solution.py:43
  65.7 2.7 %multiply_convert_fusion.2 = bf16[2,256,512]{2,1,0:T(8,128)(2,1)} fusion(bf16[256,2,512]{2,1,0:T(2,128)(2,1)} %gather_fusion.12, bf16[256,2,512]{2,1,0:T(2,128)(2,1)} %gather_fusion.11, bf16[256,2,512]{2,1,0:T(2,128)(2,1)} %gather_fusion.10, bf16[256,2,512]{2,1,0:T(2,128)(2,1)S(1)} %gather_fusion.9, bf16[256,2,512]{2,1,0:T(2,128)(2,1)S(1)} %gather_fusion.8, ...), kind=kLoop, calls=%fused_computation.43 | loop fusion | flops 4980736 | bytes 3671552 | tf_op jit(solution)/shard_map/convert_element_type | solution.py:46
  68.5 3.1 %multiply_reduce_fusion.1 = (f32[2,256]{1,0:T(2,128)S(1)}, f32[2,256,512]{2,1,0:T(8,128)S(1)}) fusion(f32[2,256,512]{2,1,0:T(8,128)} %copy-done.2, bf16[2,512,512]{2,1,0:T(8,128)(2,1)} %param.21, bf16[2,1024,512]{2,1,0:T(8,128)(2,1)} %param.20, bf16[2,256,512]{2,1,0:T(8,128)(2,1)} %multiply_convert_fusion.2, bf16[2,256,512]{2,1,0:T(8,128)(2,1)S(1)} %multiply_convert_fusion.3), kind=kOutput, calls=%fused_computation.40 | convolution fusion | flops 809500160 | bytes 4720640 | tf_op jit(solution)/shard_map/mrk,kl->mrl/dot_general | solution.py:53
  72.1 3.6 %gather_fusion = f32[1024,2,83]{2,1,0:T(2,128)S(1)} fusion(f32[2,83,256]{1,0,2:T(2,128)S(1)} %copy.202, s32[1024]{0:T(1024)S(1)} %fusion.54), kind=kCustom, calls=%fused_computation.12 | custom fusion | bytes 1363968 | tf_op jit(solution)/shard_map/jit(_take)/gather | solution.py:115
  77.3 10.6 %all-to-all-start = ((bf16[2,83,8,128]{3,0,1,2:T(2,128)(2,1)}), bf16[2,83,8,128]{3,0,1,2:T(2,128)(2,1)S(1)}, u32[]{:S(2)}, u32[]{:S(2)}) async-start(bf16[2,83,8,128]{3,0,1,2:T(2,128)(2,1)} %copy.204), calls=%async_computation | async-start | bytes 679936 | tf_op jit(solution)/shard_map/all_to_all | solution.py:125
  89.3 8.3 %all-to-all-done = bf16[2,83,8,128]{3,0,1,2:T(2,128)(2,1)S(1)} async-done(((bf16[2,83,8,128]{3,0,1,2:T(2,128)(2,1)}), bf16[2,83,8,128]{3,0,1,2:T(2,128)(2,1)S(1)}, u32[]{:S(2)}, u32[]{:S(2)}) %all-to-all-start) | async-done | bytes 340000 | tf_op jit(solution)/shard_map/all_to_all | solution.py:125
  98.2 8.9 %while.11 = (s32[]{:T(128)}, f32[16,83,128]{2,1,0:T(8,128)S(1)}, bf16[16,83,128]{2,1,0:T(8,128)(2,1)S(1)}, f32[16,83,128]{2,1,0:T(8,128)S(1)}, s32[]{:T(128)}, /*index=5*/s32[]{:T(128)}) while((s32[]{:T(128)}, f32[16,83,128]{2,1,0:T(8,128)S(1)}, bf16[16,83,128]{2,1,0:T(8,128)(2,1)S(1)}, f32[16,83,128]{2,1,0:T(8,128)S(1)}, ...), condition=%wide.region_6.8_spmd.clone, body=%wide.region_4.7_spmd.clone.sunk | while | flops 1200515 | bytes 2901331 | solution.py:63
  107.6 17.5 %all_to_all.30 = bf16[16,83,1,128]{3,1,2,0:T(8,128)(2,1)S(1)} all-to-all(bf16[16,83,1,128]{3,1,2,0:T(8,128)(2,1)S(1)} %copy.212), channel_id=1, replica_groups=mesh['member'=8,'node'=64] {'member'}, dimensions={0} | all-to-all | bytes 679936 | tf_op jit(solution)/shard_map/all_to_all | solution.py:134
  125.7 1.4 %convolution_convert_fusion = bf16[2,256,512]{2,1,0:T(8,128)(2,1)} fusion(f32[2,83,256]{2,1,0:T(8,128)S(1)} %fusion.16, bf16[83,512]{1,0:T(8,128)(2,1)S(1)} %copy-done), kind=kOutput, calls=%fused_computation.21 | convolution fusion | flops 261357568 | bytes 779264 | tf_op jit(solution)/shard_map/mcn,cl->mnl/dot_general | solution.py:151
  (131 shorter events, 16.8 us)
Async XLA Ops:
  0.6 70.9 %copy-start = (bf16[83,512]{1,0:T(8,128)(2,1)S(1)}, bf16[83,512]{1,0:T(8,128)(2,1)}, u32[]{:S(2)}) copy-start(bf16[83,512]{1,0:T(8,128)(2,1)} %param.23) | copy-start | bytes 254980
  0.6 15.9 %copy-start.7 = (f32[2,32]{1,0:T(2,128)S(1)}, f32[2,32]{1,0:T(2,128)}, u32[]{:S(2)}) copy-start(f32[2,32]{1,0:T(2,128)} %param.17) | copy-start | bytes 772
  0.7 15.9 %copy-start.5 = (f32[2,32,512]{2,1,0:T(8,128)S(1)}, f32[2,32,512]{2,1,0:T(8,128)}, u32[]{:S(2)}) copy-start(f32[2,32,512]{2,1,0:T(8,128)} %param.19) | copy-start | bytes 393220
  0.7 16.0 %copy-start.6 = (s32[6,256]{1,0:T(8,128)S(1)}, s32[6,256]{1,0:T(8,128)}, u32[]{:S(2)}) copy-start(s32[6,256]{1,0:T(8,128)} %param.18) | copy-start | bytes 18436
  0.7 16.2 %copy-start.4 = (bf16[83,1024]{1,0:T(8,128)(2,1)S(1)}, bf16[83,1024]{1,0:T(8,128)(2,1)}, u32[]{:S(2)}) copy-start(bf16[83,1024]{1,0:T(8,128)(2,1)} %param.25) | copy-start | bytes 509956
  2.0 15.0 %copy-start.8 = (s32[1024]{0:T(1024)S(1)}, s32[1024]{0:T(1024)}, u32[]{:S(2)}) copy-start(s32[1024]{0:T(1024)} %param.24) | copy-start | bytes 12292
  4.3 13.6 %collective-permute-start = (bf16[2,96,512]{2,1,0:T(8,128)(2,1)S(1)}, bf16[2,96,512]{2,1,0:T(8,128)(2,1)S(1)}, u32[]{:S(2)}, u32[]{:S(2)}) collective-permute-start(bf16[2,96,512]{2,1,0:T(8,128)(2,1)S(1)} %get-tuple-element.87), channel_id=1, source_target_pairs={{0,1},{1,2},{2,3},{3,4},{4,5},{5,6},{6,7},{7,8},{8,9},{9,10},{10,1... | collective-permute-start | bytes 589832 | tf_op jit(solution)/shard_map/ppermute | solution.py:20
  6.2 13.4 %collective-permute-start.1 = (bf16[2,96,512]{2,1,0:T(8,128)(2,1)S(1)}, bf16[2,96,512]{2,1,0:T(8,128)(2,1)S(1)}, u32[]{:S(2)}, u32[]{:S(2)}) collective-permute-start(bf16[2,96,512]{2,1,0:T(8,128)(2,1)S(1)} %get-tuple-element.88), channel_id=1, source_target_pairs={{1,0},{2,1},{3,2},{4,3},{5,4},{6,5},{7,6},{8,7},{9,8},{10,9},{11,1... | collective-permute-start | bytes 589832 | tf_op jit(solution)/shard_map/ppermute | solution.py:22
  33.4 2.8 %copy-start.1 = (bf16[2,256,512]{2,1,0:T(8,128)(2,1)S(1)}, bf16[2,256,512]{2,1,0:T(8,128)(2,1)}, u32[]{:S(2)}) copy-start(bf16[2,256,512]{2,1,0:T(8,128)(2,1)} %param.16) | copy-start | bytes 1572868
  38.9 13.0 %copy-start.2 = (f32[2,256,512]{2,1,0:T(8,128)}, f32[2,256,512]{2,1,0:T(8,128)S(1)}, u32[]{:S(2)}) copy-start(f32[2,256,512]{2,1,0:T(8,128)S(1)} %get-tuple-element.96) | copy-start | bytes 3145732
  39.1 11.1 %collective-permute-start.2 = (bf16[2,96,512]{2,1,0:T(8,128)(2,1)S(1)}, bf16[2,96,512]{2,1,0:T(8,128)(2,1)S(1)}, u32[]{:S(2)}, u32[]{:S(2)}) collective-permute-start(bf16[2,96,512]{2,1,0:T(8,128)(2,1)S(1)} %get-tuple-element.85), channel_id=1, source_target_pairs={{0,1},{1,2},{2,3},{3,4},{4,5},{5,6},{6,7},{7,8},{8,9},{9,10},{10,1... | collective-permute-start | bytes 589832 | tf_op jit(solution)/shard_map/ppermute | solution.py:20
  41.1 10.9 %collective-permute-start.3 = (bf16[2,96,512]{2,1,0:T(8,128)(2,1)S(1)}, bf16[2,96,512]{2,1,0:T(8,128)(2,1)S(1)}, u32[]{:S(2)}, u32[]{:S(2)}) collective-permute-start(bf16[2,96,512]{2,1,0:T(8,128)(2,1)S(1)} %get-tuple-element.86), channel_id=1, source_target_pairs={{1,0},{2,1},{3,2},{4,3},{5,4},{6,5},{7,6},{8,7},{9,8},{10,9},{11,1... | collective-permute-start | bytes 589832 | tf_op jit(solution)/shard_map/ppermute | solution.py:22
  68.5 3.1 %copy-start.9 = (f32[512]{0:T(512)S(1)}, f32[512]{0:T(512)}, u32[]{:S(2)}) copy-start(f32[512]{0:T(512)} %param.22) | copy-start | bytes 6148
  77.3 20.4 %all-to-all-start = ((bf16[2,83,8,128]{3,0,1,2:T(2,128)(2,1)}), bf16[2,83,8,128]{3,0,1,2:T(2,128)(2,1)S(1)}, u32[]{:S(2)}, u32[]{:S(2)}) async-start(bf16[2,83,8,128]{3,0,1,2:T(2,128)(2,1)} %copy.204), calls=%async_computation | async-start | bytes 679936 | tf_op jit(solution)/shard_map/all_to_all | solution.py:125
  125.2 1.9 %copy-start.3 = (bf16[2,83,1024]{2,0,1:T(2,128)(2,1)}, bf16[2,83,1024]{2,0,1:T(2,128)(2,1)S(1)}, u32[]{:S(2)}) copy-start(bf16[2,83,1024]{2,0,1:T(2,128)(2,1)S(1)} %reshape.92) | copy-start | bytes 1019908
where the time goes:
time: 128 us; the launch traced here: 127 us
  local copies, waits for them, and re-layouts  34.3 us (27%)
  starting transfers between devices  32.6 us (25%)
  other arithmetic  17.8 us (14%)
  blocking collectives  17.5 us (14%)
  waiting for transfers between devices  13.9 us (11%)
  matrix products  9.18 us (7%)
    gather x12, local copies, waits for them, and re-layouts, neighbour_mean(): jnp.take(normalized_rows, margin + positions + offsets, axis=1)  25.4 us
    ppermute x2, starting transfers between devices, extended(): lax.ppermute(head, axis, [((i + 1) % count, i) for i in range(count)])  18.1 us
    all_to_all x1, blocking collectives, per_device(): lax.all_to_all(patch_grad.reshape(ensemble, variable_total, 1, section_ro...  17.5 us
    all_to_all x1, starting transfers between devices, per_device(): lax.all_to_all(partition_pieces, 'member', split_axis=2, concat_axis=0, t...  10.6 us
    all_to_all x1, waiting for transfers between devices, per_device(): lax.all_to_all(partition_pieces, 'member', split_axis=2, concat_axis=0, t...  8.34 us
    add x16, other arithmetic, add_pull(): return (carried + offset / spread, None)  6.42 us
    dot_general x2, matrix products, layer_update(): jnp.einsum('mrk,kl->mrl', activated, w_out_layer, preferred_element_type=...  5.79 us
    convert_element_type x2, other arithmetic, neighbour_mean(): return (summed / mesh_links.shape[0]).astype(jnp.bfloat16)  5.53 us
  transfers between devices with their start and end apart: 5, of which 5 were waited for; matrix products, arithmetic and copies ran while one was open for 1% of the time, Pallas kernels for 0%

commit v1 on v0

v1 whole, which is shorter than its diff:
```python
import functools

import jax
import jax.numpy as jnp
from jax import lax
from jax.experimental import pallas as pl
from jax.experimental.pallas import tpu as pltpu
from jax.sharding import PartitionSpec as P

WIN = 96
NORM_EPS = 1e-06
DIST_EPS = 1e-06

BF = jnp.bfloat16
F32 = jnp.float32
VMEM = pl.BlockSpec(memory_space=pltpu.VMEM)
SMEM = pl.BlockSpec(memory_space=pltpu.SMEM)
PARAMS = pltpu.CompilerParams(vmem_limit_bytes=40 * 2**20)


def dot(lhs, rhs):
    return jnp.dot(lhs, rhs, preferred_element_type=F32)


def dot_nt(lhs, rhs):
    return lax.dot_general(lhs, rhs, (((1,), (1,)), ((), ())), preferred_element_type=F32)


def norm(values, scaling):
    inverse = lax.rsqrt(jnp.mean(values * values, axis=-1, keepdims=True) + NORM_EPS)
    return (values * inverse * scaling).astype(BF)


def silu(values):
    half = 0.5 * values
    return half + half * jnp.tanh(half)


def parts_of(values, count):
    parts = []
    for _ in range(count):
        part = values.astype(BF)
        parts.append(part)
        values = values - part.astype(F32)
    return parts


def padded(rows):
    return -(-rows // 256) * 256


def gains(noise_ref, w_cond_ref, layer):
    return 1.0 + jnp.dot(
        noise_ref[...], w_cond_ref[layer], precision=lax.Precision.HIGHEST, preferred_element_type=F32
    )


def link_offsets(links, first, node_total):
    own = first + lax.broadcasted_iota(jnp.int32, links.shape, 1)
    away = links - own
    away = jnp.where(away > node_total // 2, away - node_total, away)
    away = jnp.where(away < -(node_total // 2), away + node_total, away)
    return away.astype(F32)


def count_matrix(offsets, width):
    link_count, rows = offsets.shape
    places = offsets + (WIN + lax.broadcasted_iota(jnp.int32, offsets.shape, 1)).astype(F32)
    places = jnp.concatenate([places, jnp.full((128 - link_count, rows), -1.0, F32)], axis=0).T
    columns = lax.broadcasted_iota(jnp.int32, (rows, width), 1).astype(F32)
    total = jnp.zeros((rows, width), F32)
    for slot in range(link_count):
        total = total + jnp.where(columns == places[:, slot : slot + 1], 1.0, 0.0)
    return total.astype(BF)


def layer(values, normed, window, counts, w_in, w_out, link_count):
    neighbours = (dot(counts, window)[: values.shape[0]] * (1.0 / link_count)).astype(BF)
    depth = normed.shape[1]
    preact = dot(normed, w_in[:depth]) + dot(neighbours, w_in[depth:])
    return values + dot(silu(preact).astype(BF), w_out)


def pack_kernel(node_total, place, latent, links, near, far):
    odd, first = place[0], place[1]
    halo = 2 * WIN
    rows = latent.shape[1]
    offsets = link_offsets(links[...], first, node_total).astype(BF)
    for send, start in ((near, (1 - odd) * (rows - halo)), (far, odd * (rows - halo))):
        start = pl.multiple_of(start, 64)
        for member in range(latent.shape[0]):
            send[member * halo : (member + 1) * halo] = latent[member, pl.ds(start, halo)]
        tail = latent.shape[0] * halo
        send[tail:] = jnp.zeros((send.shape[0] - tail, send.shape[1]), BF)
        send[tail : tail + offsets.shape[0], : offsets.shape[1]] = offsets


def received_offsets(received, tail, link_count, rows):
    return received[tail : tail + 16, :rows].astype(F32)[:link_count]


def near_kernel(
    node_total, place, latent, links, near, noise, w_cond, w_in, w_out,
    state_out, normed_own_out, normed_next_out, counts_out, window, inputs
):
    odd, first = place[0], place[1]
    members, rows, _ = latent.shape
    link_count = links.shape[0]
    halo = 2 * WIN
    own_at = pl.multiple_of(odd * halo, 64)
    near_at = pl.multiple_of((1 - odd) * rows, 64)
    scaling = gains(noise, w_cond, 0)
    next_scaling = gains(noise, w_cond, 1)
    own_offsets = link_offsets(links[...], first, node_total)
    near_offsets = received_offsets(near, members * halo, link_count, rows)
    lane = lax.broadcasted_iota(jnp.int32, own_offsets.shape, 1)
    mine = jnp.logical_and(lane >= (1 - odd) * WIN, lane < rows - odd * WIN)
    mixed = jnp.where(mine, own_offsets, near_offsets)
    mixed = pltpu.roll(mixed, rows - WIN - odd * (rows - 2 * WIN), 1)
    counts = count_matrix(mixed, window.shape[1])
    counts_out[...] = count_matrix(own_offsets, window.shape[1])
    for member in range(members):
        scale = scaling[member : member + 1]
        own = latent[member]
        edge = near[member * halo : (member + 1) * halo]
        inputs[member, pl.ds(own_at, rows)] = own
        inputs[member, pl.ds(near_at, halo)] = edge
        normed_own = norm(own.astype(F32), scale)
        normed_own_out[member] = normed_own
        window[member, rows + halo :] = jnp.zeros((window.shape[1] - rows - halo, window.shape[2]), BF)
        window[member, pl.ds(own_at, rows)] = normed_own
        window[member, pl.ds(near_at, halo)] = norm(edge.astype(F32), scale)
        values = inputs[member, WIN : WIN + rows].astype(F32)
        values = layer(
            values, window[member, WIN : WIN + rows], window[member], counts, w_in[0], w_out[0], link_count
        )
        state_out[member] = values
        normed_next_out[member] = norm(values, next_scaling[member : member + 1])


def far_kernel(
    node_total, copies, place, latent, links, far, noise, w_cond, w_in, w_out, dec_gain, w_dec,
    state_in, normed_own, normed_next, counts_own, decoded_out, send_out,
    window, inputs, state, window_next, features,
):
    odd, first = place[0], place[1]
    members, rows, _ = latent.shape
    link_count = links.shape[0]
    halo = 2 * WIN
    even = 1 - odd
    scaling = gains(noise, w_cond, 0)
    next_scaling = gains(noise, w_cond, 1)
    own_offsets = link_offsets(links[...], first, node_total)
    far_offsets = received_offsets(far, members * halo, link_count, rows)
    lane = lax.broadcasted_iota(jnp.int32, own_offsets.shape, 1)
    mine = jnp.logical_or(
        jnp.logical_and(odd == 0, lane < WIN), jnp.logical_and(odd == 1, lane >= rows - WIN)
    )
    counts = count_matrix(pltpu.roll(jnp.where(mine, own_offsets, far_offsets), WIN, 1), window.shape[1])
    filled = rows + halo
    for member in range(members):
        window[member, 2 * halo :] = jnp.zeros((window.shape[1] - 2 * halo, window.shape[2]), BF)
        window_next[member, filled:] = jnp.zeros((window_next.shape[1] - filled, window_next.shape[2]), BF)
        edge = far[member * halo : (member + 1) * halo]
        window[member, pl.ds(pl.multiple_of(odd * halo, 64), halo)] = norm(
            edge.astype(F32), scaling[member : member + 1]
        )
        window[member, pl.ds(pl.multiple_of(even * halo, 64), halo)] = normed_own[
            member, pl.ds(pl.multiple_of(odd * (rows - halo), 64), halo)
        ]
        inputs[member, pl.ds(pl.multiple_of(odd * WIN, 32), WIN)] = far[
            pl.ds(pl.multiple_of(member * halo + even * WIN, 32), WIN)
        ]
        inputs[member, pl.ds(pl.multiple_of(even * WIN, 32), WIN)] = latent[
            member, pl.ds(pl.multiple_of(odd * (rows - WIN), 32), WIN)
        ]
        values = layer(
            inputs[member].astype(F32), window[member, WIN : WIN + halo], window[member], counts, w_in[0], w_out[0], link_count
        )
        far_at = pl.multiple_of(odd * rows, 64)
        near_at = pl.multiple_of(even * halo, 64)
        state[member, pl.ds(far_at, halo)] = values
        state[member, pl.ds(near_at, rows)] = state_in[member]
        window_next[member, pl.ds(far_at, halo)] = norm(values, next_scaling[member : member + 1])
        window_next[member, pl.ds(near_at, rows)] = normed_next[member]
        values = layer(
            state[member, WIN : WIN + rows], window_next[member, WIN : WIN + rows], window_next[member], counts_own[...],
            w_in[1], w_out[1], link_count,
        )
        features[member * rows : (member + 1) * rows] = norm(values, dec_gain[...])
    decoded = dot_nt(w_dec[...], features[...])
    decoded_out[...] = decoded
    rounded = decoded.astype(BF)
    for copy in range(copies):
        send_out[copy] = rounded


def grid_kernel(ensemble, place, decoded, prior, target, vertex, weight, incidence_out, base_out):
    nodes, points = incidence_out.shape
    ids = place[1] + lax.broadcasted_iota(jnp.int32, (nodes, points), 0)
    incidence = jnp.where(ids == vertex[...], 1.0, 0.0).astype(BF)
    incidence_out[...] = incidence
    before = prior[...].astype(F32)
    truth = target[...].astype(F32)
    for member in range(base_out.shape[0]):
        own = decoded[:, member * nodes : (member + 1) * nodes]
        at_points = sum(dot(part, incidence) for part in parts_of(own, 3)[::-1])
        missed = (before + at_points).astype(BF).astype(F32) - truth
        reached = lax.rsqrt(jnp.sum(missed * missed, axis=0, keepdims=True) + DIST_EPS)
        base_out[member] = missed * (reached * weight[...] * (1.0 / ensemble))


def score_kernel(ensemble, decoded, others, incidence, base, weight, w_dec, grad_out, vertex_out):
    members, channels, _ = base.shape
    nodes = incidence.shape[0]
    factor = weight[...] * (1.0 / (ensemble * (ensemble - 1)))
    step = 128
    for member in range(members):
        pulls = []
        for start in range(member * nodes, (member + 1) * nodes, step):
            anchor = decoded[:, start : start + step].astype(BF).astype(F32)
            total = jnp.zeros_like(anchor)
            for group in range(others.shape[0]):
                for at in range(start % nodes, members * nodes, nodes):
                    offset = anchor - others[group, :, at : at + step].astype(F32)
                    near = jnp.sum(offset * offset, axis=0, keepdims=True) + DIST_EPS
                    total = total + offset * lax.rsqrt(near)
            pulls.append(total)
        pull = jnp.concatenate(pulls, axis=1)
        at_points = sum(dot(part, incidence[...]) for part in parts_of(pull, 2)[::-1])
        grad = (base[member] - factor * at_points).astype(BF)
        grad_out[member] = grad
        by_node = dot_nt(incidence[...], grad)
        vertex_out[member] = sum(dot(part, w_dec[...]) for part in parts_of(by_node, 3)[::-1]).astype(BF)


def call(kernel, outs, count, scratch=(), place=True):
    return pl.pallas_call(
        kernel,
        out_shape=[jax.ShapeDtypeStruct(shape, kind) for shape, kind in outs],
        in_specs=[SMEM] * place + [VMEM] * count,
        out_specs=[VMEM] * len(outs),
        scratch_shapes=[pltpu.VMEM(shape, kind) for shape, kind in scratch],
        compiler_params=PARAMS,
    )


def per_device(
    latent, noise_draw, mesh_links, w_cond, w_in, w_out, dec_gain, w_dec,
    target_vertex_map, prior_field, target, location_loss_factor,
):
    members, rows, depth = latent.shape
    channels, points = prior_field.shape
    shards = lax.axis_size("node")
    groups = lax.axis_size("member")
    ensemble = members * groups
    node_total = rows * shards
    halo = 2 * WIN
    wide = padded(rows + halo)
    shard = lax.axis_index("node")
    place = jnp.stack([shard % 2, shard * rows]).astype(jnp.int32)
    sent = (members * halo + 16, depth)
    near_pairs = [(i, i ^ 1) for i in range(shards)]
    far_pairs = [(i, (i + 1) % shards if i % 2 else (i - 1) % shards) for i in range(shards)]

    near, far = call(functools.partial(pack_kernel, node_total), [(sent, BF)] * 2, 2)(place, latent, mesh_links)
    far = lax.ppermute(far, "node", far_pairs)
    near = lax.ppermute(near, "node", near_pairs)
    state, normed_own, normed_next, counts_own = call(
        functools.partial(near_kernel, node_total),
        [
            ((members, rows, depth), F32),
            ((members, rows, depth), BF),
            ((members, rows, depth), BF),
            ((rows, wide), BF),
        ],
        7,
        [((members, wide, depth), BF), ((members, rows + halo, depth), BF)],
    )(place, latent, mesh_links, near, noise_draw, w_cond, w_in, w_out)
    decoded, send = call(
        functools.partial(far_kernel, node_total, groups),
        [((channels, members * rows), F32), ((groups, channels, members * rows), BF)],
        13,
        [
            ((members, padded(2 * halo), depth), BF),
            ((members, halo, depth), BF),
            ((members, rows + halo, depth), F32),
            ((members, wide, depth), BF),
            ((members * rows, depth), BF),
        ],
    )(
        place, latent, mesh_links, far, noise_draw, w_cond, w_in, w_out, dec_gain.reshape(1, depth), w_dec,
        state, normed_own, normed_next, counts_own,
    )
    others = lax.all_to_all(send, "member", split_axis=0, concat_axis=0, tiled=True)
    weight = location_loss_factor.reshape(1, points)
    incidence, base = call(
        functools.partial(grid_kernel, ensemble),
        [((rows, points), BF), ((members, channels, points), F32)],
        5,
    )(place, decoded, prior_field, target, target_vertex_map.reshape(1, points), weight)
    prediction_sensitivity, vertex_attribute_sensitivity = call(
        functools.partial(score_kernel, ensemble),
        [((members, channels, points), BF), ((members, rows, depth), BF)],
        6,
        place=False,
    )(decoded, others, incidence, base, weight, w_dec)
    return prediction_sensitivity, vertex_attribute_sensitivity


def solution(mesh):
    in_specs = (
        P("member", "node", None),
        P("member", None),
        P(None, "node"),
        P(),
        P(),
        P(),
        P(),
        P(),
        P("node"),
        P(None, "node"),
        P(None, "node"),
        P("node"),
    )
    out_specs = (P("member", None, "node"), P("member", "node", None))
    return jax.shard_map(
        per_device, mesh=mesh, in_specs=in_specs, out_specs=out_specs, check_vma=False
    )
```

time: 128 us -> 63.2 us (0.49)
  the two profiles are of different devices: /device:TPU:2 before, /device:TPU:120 now
where the time goes in v1:
time: 63.2 us; the launch traced here: 62.8 us
  waiting for transfers between devices  23.5 us (37%)
  starting transfers between devices  17.1 us (27%)
  Pallas kernels  14.1 us (22%)
  local copies, waits for them, and re-layouts  7.25 us (11%)
  between operations  0.81 us (1%)
    all_to_all x1, waiting for transfers between devices, per_device(): lax.all_to_all(send, 'member', split_axis=0, concat_axis=0, tiled=True)  23.5 us
    all_to_all x1, starting transfers between devices, per_device(): lax.all_to_all(send, 'member', split_axis=0, concat_axis=0, tiled=True)  11.8 us
    unnamed x28, local copies, waits for them, and re-layouts  6.17 us
    pallas_call x1, Pallas kernels, per_device(): call(functools.partial(far_kernel, node_total, groups), [((channels, memb...  5.85 us
    ppermute x1, starting transfers between devices, per_device(): far = lax.ppermute(far, 'node', far_pairs)  3.36 us
    pallas_call x1, Pallas kernels, per_device(): call(functools.partial(near_kernel, node_total), [((members, rows, depth)...  3.21 us
    pallas_call x1, Pallas kernels, per_device(): call(functools.partial(score_kernel, ensemble), [((members, channels, poi...  3.09 us
    ppermute x1, starting transfers between devices, per_device(): near = lax.ppermute(near, 'node', near_pairs)  1.92 us
  transfers between devices with their start and end apart: 3, of which 1 were waited for; matrix products, arithmetic and copies ran while one was open for 0% of the time, Pallas kernels for 7%

profile of v1, /device:TPU:120, one launch (start us, length us, event | category | flops | bytes accessed | tf_op | source)
XLA Modules:
  0.0 62.8 jit_solution(2182542970471780432)
XLA Ops:
  0.6 0.1 pad_add_fusion.place
  0.7 1.0 %copy-done.2 = bf16[2,256,512]{2,1,0:T(8,128)(2,1)S(1)} copy-done((bf16[2,256,512]{2,1,0:T(8,128)(2,1)S(1)}, bf16[2,256,512]{2,1,0:T(8,128)(2,1)}, u32[]{:S(2)}) %copy-start.2) | copy-done | bytes 524312
  1.8 0.7 %copy-done.9 = s32[6,256]{1,0:T(8,128)S(1)} copy-done((s32[6,256]{1,0:T(8,128)S(1)}, s32[6,256]{1,0:T(8,128)}, u32[]{:S(2)}) %copy-start.9) | copy-done | bytes 6168
  2.5 0.6 shard_map.131
  3.1 1.9 %collective-permute-start.1 = (bf16[400,512]{1,0:T(8,128)(2,1)S(1)}, bf16[400,512]{1,0:T(8,128)(2,1)S(1)}, u32[]{:S(2)}, u32[]{:S(2)}) collective-permute-start(bf16[400,512]{1,0:T(8,128)(2,1)S(1)} %get-tuple-element.13), channel_id=1, source_target_pairs={{0,1},{1,0},{2,3},{3,2},{4,5},{5,4},{6,7},{7,6},{8,9},{9,8},{10,11... | collective-permute-start | bytes 1228808 | tf_op jit(solution)/shard_map/ppermute | solution.py:268
  5.0 3.4 %collective-permute-start = (bf16[400,512]{1,0:T(8,128)(2,1)S(1)}, bf16[400,512]{1,0:T(8,128)(2,1)S(1)}, u32[]{:S(2)}, u32[]{:S(2)}) collective-permute-start(bf16[400,512]{1,0:T(8,128)(2,1)S(1)} %get-tuple-element.12), channel_id=1, source_target_pairs={{0,63},{1,2},{2,1},{3,4},{4,3},{5,6},{6,5},{7,8},{8,7},{9,10},{10,... | collective-permute-start | bytes 1228808 | tf_op jit(solution)/shard_map/ppermute | solution.py:267
  8.4 0.0 collective-permute-done.1.near
  8.4 0.0 copy-start
  8.4 1.6 %copy-done = bf16[2,1024,512]{2,1,0:T(8,128)(2,1)S(1)} copy-done((bf16[2,1024,512]{2,1,0:T(8,128)(2,1)S(1)}, bf16[2,1024,512]{2,1,0:T(8,128)(2,1)}, u32[]{:S(2)}) %copy-start) | copy-done | bytes 2097176
  10.0 1.2 %copy-done.3 = bf16[2,512,512]{2,1,0:T(8,128)(2,1)S(1)} copy-done((bf16[2,512,512]{2,1,0:T(8,128)(2,1)S(1)}, bf16[2,512,512]{2,1,0:T(8,128)(2,1)}, u32[]{:S(2)}) %copy-start.3) | copy-done | bytes 1048600
  11.2 0.9 %copy-done.5 = f32[2,32,512]{2,1,0:T(8,128)S(1)} copy-done((f32[2,32,512]{2,1,0:T(8,128)S(1)}, f32[2,32,512]{2,1,0:T(8,128)}, u32[]{:S(2)}) %copy-start.5) | copy-done | bytes 131096
  12.1 0.7 %copy-done.12 = f32[2,32]{1,0:T(2,128)S(1)} copy-done((f32[2,32]{1,0:T(2,128)S(1)}, f32[2,32]{1,0:T(2,128)}, u32[]{:S(2)}) %copy-start.12) | copy-done | bytes 280
  12.8 3.2 %shard_map.132 = (f32[2,256,512]{2,1,0:T(8,128)S(1)}, bf16[2,256,512]{2,1,0:T(8,128)(2,1)S(1)}, bf16[2,256,512]{2,1,0:T(8,128)(2,1)S(1)}, bf16[256,512]{1,0:T(8,128)(2,1)S(1)}) custom-call(s32[2]{0:T(128)S(1)} %pad_add_fusion.place, bf16[2,256,512]{2,1,0:T(8,128)(2,1)S(1)} %copy-done.2, s32[6,256]{1,0:T(8,128)S(1)} %copy-done.9, ...), custom_call_target="tpu_custom_call" | custom-call | tf_op jit(solution)/shard_map/pallas_call | solution.py:269
  16.0 0.0 collective-permute-done.far
  16.0 0.0 copy-done.1
  16.0 0.0 copy-done.4
  16.0 0.0 copy-done.6
  16.0 0.0 copy-done.13
  16.0 0.0 copy-start.7
  16.1 0.0 copy-start.8
  16.1 0.0 copy-start.10
  16.1 0.0 copy-start.11
  16.1 5.9 %shard_map.133 = (f32[83,512]{1,0:T(8,128)S(1)}, bf16[8,83,512]{2,1,0:T(8,128)(2,1)}) custom-call(s32[2]{0:T(128)S(1)} %pad_add_fusion.place, bf16[2,256,512]{2,1,0:T(8,128)(2,1)S(1)} %copy-done.2, s32[6,256]{1,0:T(8,128)S(1)} %copy-done.9, bf16[400,512]{1,0:T(8,128)(2,1)S(1)} %collective-permute-done.far, f32[2,32]{1,0:T(2,128)S(1)} %copy-done.12, ...), custom_call_target="tpu_custom_call" | custom-call | tf_op jit(solution)/shard_map/pallas_call | solution.py:280
  21.9 11.8 %all-to-all-start = ((bf16[8,83,512]{2,1,0:T(8,128)(2,1)}), bf16[8,83,512]{2,1,0:T(8,128)(2,1)S(1)}, u32[]{:S(2)}, u32[]{:S(2)}) async-start(bf16[8,83,512]{2,1,0:T(8,128)(2,1)} %get-tuple-element.19), calls=%async_computation | async-start | bytes 1441792 | tf_op jit(solution)/shard_map/all_to_all | solution.py:295
  33.8 0.0 copy-done.7
  33.8 0.0 copy-done.8
  33.8 0.0 copy-done.10
  33.8 0.0 copy-done.11
  33.8 1.4 %shard_map.134 = (bf16[256,1024]{1,0:T(8,128)(2,1)S(1)}, f32[2,83,1024]{2,1,0:T(8,128)S(1)}) custom-call(s32[2]{0:T(128)S(1)} %pad_add_fusion.place, f32[83,512]{1,0:T(8,128)S(1)} %get-tuple-element.18.decoded, bf16[83,1024]{1,0:T(8,128)(2,1)S(1)} %copy-done.7, bf16[83,1024]{1,0:T(8,128)(2,1)S(1)} %copy-done.8, s32[1,1024]{1,0:T(1,128)S(1)} %bitcast.7, ...), custom_call_target="tpu_custom_call" | custom-call | tf_op jit(solution)/shard_map/pallas_call | solution.py:297
  35.2 23.5 %all-to-all-done.others = bf16[8,83,512]{2,1,0:T(8,128)(2,1)S(1)} async-done(((bf16[8,83,512]{2,1,0:T(8,128)(2,1)}), bf16[8,83,512]{2,1,0:T(8,128)(2,1)S(1)}, u32[]{:S(2)}, u32[]{:S(2)}) %all-to-all-start) | async-done | bytes 679968 | tf_op jit(solution)/shard_map/all_to_all | solution.py:295
  58.7 3.1 %shard_map.135 = (bf16[2,83,1024]{2,1,0:T(8,128)(2,1)S(1)}, bf16[2,256,512]{2,1,0:T(8,128)(2,1)}) custom-call(f32[83,512]{1,0:T(8,128)S(1)} %get-tuple-element.18.decoded, bf16[8,83,512]{2,1,0:T(8,128)(2,1)S(1)} %all-to-all-done.others, bf16[256,1024]{1,0:T(8,128)(2,1)S(1)} %get-tuple-element.20.incidence, f32[2,83,1024]{2,1,0:T(8,128)S(1)} %get-tuple-element.21.base, ...), custom_call_target="tpu_custom_call" | custom-call | tf_op jit(solution)/shard_map/pallas_call | solution.py:302
  61.7 1.1 %copy.14 = bf16[2,83,1024]{2,0,1:T(2,128)(2,1)} copy(bf16[2,83,1024]{2,1,0:T(8,128)(2,1)S(1)} %get-tuple-element.22) | data formatting | bytes 679936 | tf_op jit(solution)/shard_map/pallas_call | solution.py:302
  (9 shorter events, 0.0 us)
Async XLA Ops:
  0.7 1.0 %copy-start.2 = (bf16[2,256,512]{2,1,0:T(8,128)(2,1)S(1)}, bf16[2,256,512]{2,1,0:T(8,128)(2,1)}, u32[]{:S(2)}) copy-start(bf16[2,256,512]{2,1,0:T(8,128)(2,1)} %latent.5) | copy-start | bytes 1572868
  1.8 0.7 %copy-start.9 = (s32[6,256]{1,0:T(8,128)S(1)}, s32[6,256]{1,0:T(8,128)}, u32[]{:S(2)}) copy-start(s32[6,256]{1,0:T(8,128)} %links.5) | copy-start | bytes 18436
  3.1 5.3 %collective-permute-start.1 = (bf16[400,512]{1,0:T(8,128)(2,1)S(1)}, bf16[400,512]{1,0:T(8,128)(2,1)S(1)}, u32[]{:S(2)}, u32[]{:S(2)}) collective-permute-start(bf16[400,512]{1,0:T(8,128)(2,1)S(1)} %get-tuple-element.13), channel_id=1, source_target_pairs={{0,1},{1,0},{2,3},{3,2},{4,5},{5,4},{6,7},{7,6},{8,9},{9,8},{10,11... | collective-permute-start | bytes 1228808 | tf_op jit(solution)/shard_map/ppermute | solution.py:268
  5.0 11.0 %collective-permute-start = (bf16[400,512]{1,0:T(8,128)(2,1)S(1)}, bf16[400,512]{1,0:T(8,128)(2,1)S(1)}, u32[]{:S(2)}, u32[]{:S(2)}) collective-permute-start(bf16[400,512]{1,0:T(8,128)(2,1)S(1)} %get-tuple-element.12), channel_id=1, source_target_pairs={{0,63},{1,2},{2,1},{3,4},{4,3},{5,6},{6,5},{7,8},{8,7},{9,10},{10,... | collective-permute-start | bytes 1228808 | tf_op jit(solution)/shard_map/ppermute | solution.py:267
  8.4 1.6 %copy-start = (bf16[2,1024,512]{2,1,0:T(8,128)(2,1)S(1)}, bf16[2,1024,512]{2,1,0:T(8,128)(2,1)}, u32[]{:S(2)}) copy-start(bf16[2,1024,512]{2,1,0:T(8,128)(2,1)} %w_in.3) | copy-start | bytes 6291460
  10.0 1.2 %copy-start.3 = (bf16[2,512,512]{2,1,0:T(8,128)(2,1)S(1)}, bf16[2,512,512]{2,1,0:T(8,128)(2,1)}, u32[]{:S(2)}) copy-start(bf16[2,512,512]{2,1,0:T(8,128)(2,1)} %w_out.3) | copy-start | bytes 3145732
  11.2 0.9 %copy-start.5 = (f32[2,32,512]{2,1,0:T(8,128)S(1)}, f32[2,32,512]{2,1,0:T(8,128)}, u32[]{:S(2)}) copy-start(f32[2,32,512]{2,1,0:T(8,128)} %w_cond.3) | copy-start | bytes 393220
  12.1 0.7 %copy-start.12 = (f32[2,32]{1,0:T(2,128)S(1)}, f32[2,32]{1,0:T(2,128)}, u32[]{:S(2)}) copy-start(f32[2,32]{1,0:T(2,128)} %noise.3) | copy-start | bytes 772
  12.8 3.2 %copy-start.1 = (bf16[2,1024,512]{2,1,0:T(8,128)(2,1)S(1)}, bf16[2,1024,512]{2,1,0:T(8,128)(2,1)}, u32[]{:S(2)}) copy-start(bf16[2,1024,512]{2,1,0:T(8,128)(2,1)} %w_in.3) | copy-start | bytes 6291460
  12.8 3.2 %copy-start.4 = (bf16[2,512,512]{2,1,0:T(8,128)(2,1)S(1)}, bf16[2,512,512]{2,1,0:T(8,128)(2,1)}, u32[]{:S(2)}) copy-start(bf16[2,512,512]{2,1,0:T(8,128)(2,1)} %w_out.3) | copy-start | bytes 3145732
  12.8 3.3 %copy-start.6 = (bf16[83,512]{1,0:T(8,128)(2,1)S(1)}, bf16[83,512]{1,0:T(8,128)(2,1)}, u32[]{:S(2)}) copy-start(bf16[83,512]{1,0:T(8,128)(2,1)} %w_dec.3) | copy-start | bytes 254980
  12.8 3.3 %copy-start.13 = (f32[512]{0:T(512)S(1)}, f32[512]{0:T(512)}, u32[]{:S(2)}) copy-start(f32[512]{0:T(512)} %param.18) | copy-start | bytes 6148
  16.0 17.7 %copy-start.7 = (bf16[83,1024]{1,0:T(8,128)(2,1)S(1)}, bf16[83,1024]{1,0:T(8,128)(2,1)}, u32[]{:S(2)}) copy-start(bf16[83,1024]{1,0:T(8,128)(2,1)} %prior.1) | copy-start | bytes 509956
  16.1 17.7 %copy-start.8 = (bf16[83,1024]{1,0:T(8,128)(2,1)S(1)}, bf16[83,1024]{1,0:T(8,128)(2,1)}, u32[]{:S(2)}) copy-start(bf16[83,1024]{1,0:T(8,128)(2,1)} %target.1) | copy-start | bytes 509956
  16.1 17.7 %copy-start.10 = (f32[1024]{0:T(1024)S(1)}, f32[1024]{0:T(1024)}, u32[]{:S(2)}) copy-start(f32[1024]{0:T(1024)} %param.23) | copy-start | bytes 12292
  16.1 17.7 %copy-start.11 = (s32[1024]{0:T(1024)S(1)}, s32[1024]{0:T(1024)}, u32[]{:S(2)}) copy-start(s32[1024]{0:T(1024)} %param.20) | copy-start | bytes 12292
  21.9 36.7 %all-to-all-start = ((bf16[8,83,512]{2,1,0:T(8,128)(2,1)}), bf16[8,83,512]{2,1,0:T(8,128)(2,1)S(1)}, u32[]{:S(2)}, u32[]{:S(2)}) async-start(bf16[8,83,512]{2,1,0:T(8,128)(2,1)} %get-tuple-element.19), calls=%async_computation | async-start | bytes 1441792 | tf_op jit(solution)/shard_map/all_to_all | solution.py:295

commit v2 on v1

--- a/solution.py
+++ b/solution.py
@@ -15,6 +15,7 @@
 F32 = jnp.float32
 VMEM = pl.BlockSpec(memory_space=pltpu.VMEM)
 SMEM = pl.BlockSpec(memory_space=pltpu.SMEM)
+HBM = pl.BlockSpec(memory_space=pltpu.HBM)
 PARAMS = pltpu.CompilerParams(vmem_limit_bytes=40 * 2**20)
 
 
@@ -81,18 +82,31 @@
     return values + dot(silu(preact).astype(BF), w_out)
 
 
-def pack_kernel(node_total, place, latent, links, near, far):
+def fetch_all(pairs, sems):
+    fetches = [pltpu.make_async_copy(there, here, sems.at[at]) for at, (there, here) in enumerate(pairs)]
+    for fetch in fetches:
+        fetch.start()
+    return fetches
+
+
+def pack_kernel(node_total, place, latent, links_in, near, far, links, sems):
     odd, first = place[0], place[1]
     halo = 2 * WIN
-    rows = latent.shape[1]
-    offsets = link_offsets(links[...], first, node_total).astype(BF)
+    members, rows, _ = latent.shape
+    pairs = [(links_in, links)]
     for send, start in ((near, (1 - odd) * (rows - halo)), (far, odd * (rows - halo))):
         start = pl.multiple_of(start, 64)
-        for member in range(latent.shape[0]):
-            send[member * halo : (member + 1) * halo] = latent[member, pl.ds(start, halo)]
-        tail = latent.shape[0] * halo
+        for member in range(members):
+            pairs.append((latent.at[member, pl.ds(start, halo)], send.at[pl.ds(member * halo, halo)]))
+    fetches = fetch_all(pairs, sems)
+    fetches[0].wait()
+    offsets = link_offsets(links[...], first, node_total).astype(BF)
+    tail = members * halo
+    for send in (near, far):
         send[tail:] = jnp.zeros((send.shape[0] - tail, send.shape[1]), BF)
         send[tail : tail + offsets.shape[0], : offsets.shape[1]] = offsets
+    for fetch in fetches[1:]:
+        fetch.wait()
 
 
 def received_offsets(received, tail, link_count, rows):
@@ -100,17 +114,28 @@
 
 
 def near_kernel(
-    node_total, place, latent, links, near, noise, w_cond, w_in, w_out,
-    state_out, normed_own_out, normed_next_out, counts_out, window, inputs
+    node_total, place, near, links_in, noise_in, w_cond_in, latent_in, w_in_in, w_out_in,
+    state_out, normed_own_out, normed_next_out, counts_out, window, inputs,
+    links, noise, w_cond, latent, w_in, w_out, sems
 ):
+    fetches = fetch_all(
+        (
+            (links_in, links),
+            (noise_in, noise),
+            (w_cond_in, w_cond),
+            (latent_in, latent),
+            (w_in_in.at[0], w_in),
+            (w_out_in.at[0], w_out),
+        ),
+        sems,
+    )
     odd, first = place[0], place[1]
     members, rows, _ = latent.shape
     link_count = links.shape[0]
     halo = 2 * WIN
     own_at = pl.multiple_of(odd * halo, 64)
     near_at = pl.multiple_of((1 - odd) * rows, 64)
-    scaling = gains(noise, w_cond, 0)
-    next_scaling = gains(noise, w_cond, 1)
+    fetches[0].wait()
     own_offsets = link_offsets(links[...], first, node_total)
     near_offsets = received_offsets(near, members * halo, link_count, rows)
     lane = lax.broadcasted_iota(jnp.int32, own_offsets.shape, 1)
@@ -119,6 +144,10 @@
     mixed = pltpu.roll(mixed, rows - WIN - odd * (rows - 2 * WIN), 1)
     counts = count_matrix(mixed, window.shape[1])
     counts_out[...] = count_matrix(own_offsets, window.shape[1])
+    for fetch in fetches[1:4]:
+        fetch.wait()
+    scaling = gains(noise, w_cond, 0)
+    next_scaling = gains(noise, w_cond, 1)
     for member in range(members):
         scale = scaling[member : member + 1]
         own = latent[member]
@@ -130,17 +159,21 @@
         window[member, rows + halo :] = jnp.zeros((window.shape[1] - rows - halo, window.shape[2]), BF)
         window[member, pl.ds(own_at, rows)] = normed_own
         window[member, pl.ds(near_at, halo)] = norm(edge.astype(F32), scale)
+    for fetch in fetches[4:]:
+        fetch.wait()
+    for member in range(members):
         values = inputs[member, WIN : WIN + rows].astype(F32)
         values = layer(
-            values, window[member, WIN : WIN + rows], window[member], counts, w_in[0], w_out[0], link_count
+            values, window[member, WIN : WIN + rows], window[member], counts,
+            w_in[...], w_out[...], link_count,
         )
         state_out[member] = values
         normed_next_out[member] = norm(values, next_scaling[member : member + 1])
 
 
 def far_kernel(
-    node_total, copies, place, latent, links, far, noise, w_cond, w_in, w_out, dec_gain, w_dec,
-    state_in, normed_own, normed_next, counts_own, decoded_out, send_out,
+    node_total, place, latent, links, far, noise, w_cond, w_in, w_out, dec_gain, w_dec,
+    state_in, normed_own, normed_next, counts_own, decoded_out, rounded_out,
     window, inputs, state, window_next, features,
 ):
     odd, first = place[0], place[1]
@@ -190,9 +223,14 @@
         features[member * rows : (member + 1) * rows] = norm(values, dec_gain[...])
     decoded = dot_nt(w_dec[...], features[...])
     decoded_out[...] = decoded
-    rounded = decoded.astype(BF)
-    for copy in range(copies):
-        send_out[copy] = rounded
+    rounded_out[...] = decoded.astype(BF)
+
+
+def stack_kernel(mine, partner, out):
+    wide = mine.shape[1]
+    for copy in range(out.shape[0]):
+        out[copy, :, :wide] = mine[...]
+        out[copy, :, wide:] = partner[...]
 
 
 def grid_kernel(ensemble, place, decoded, prior, target, vertex, weight, incidence_out, base_out):
@@ -210,18 +248,21 @@
         base_out[member] = missed * (reached * weight[...] * (1.0 / ensemble))
 
 
-def score_kernel(ensemble, decoded, others, incidence, base, weight, w_dec, grad_out, vertex_out):
+def score_kernel(
+    ensemble, rounded, others, incidence, base, weight, w_dec, grad_out, vertex_out, grads, vertices, sems
+):
     members, channels, _ = base.shape
     nodes = incidence.shape[0]
     factor = weight[...] * (1.0 / (ensemble * (ensemble - 1)))
     step = 128
+    copies = []
     for member in range(members):
         pulls = []
         for start in range(member * nodes, (member + 1) * nodes, step):
-            anchor = decoded[:, start : start + step].astype(BF).astype(F32)
+            anchor = rounded[:, start : start + step].astype(F32)
             total = jnp.zeros_like(anchor)
             for group in range(others.shape[0]):
-                for at in range(start % nodes, members * nodes, nodes):
+                for at in range(start % nodes, others.shape[2], nodes):
                     offset = anchor - others[group, :, at : at + step].astype(F32)
                     near = jnp.sum(offset * offset, axis=0, keepdims=True) + DIST_EPS
                     total = total + offset * lax.rsqrt(near)
@@ -229,18 +270,24 @@
         pull = jnp.concatenate(pulls, axis=1)
         at_points = sum(dot(part, incidence[...]) for part in parts_of(pull, 2)[::-1])
         grad = (base[member] - factor * at_points).astype(BF)
-        grad_out[member] = grad
+        grads[member] = grad
+        copies.append(pltpu.make_async_copy(grads.at[member], grad_out.at[member], sems.at[0, member]))
+        copies[-1].start()
         by_node = dot_nt(incidence[...], grad)
-        vertex_out[member] = sum(dot(part, w_dec[...]) for part in parts_of(by_node, 3)[::-1]).astype(BF)
-
-
-def call(kernel, outs, count, scratch=(), place=True):
+        vertices[member] = sum(dot(part, w_dec[...]) for part in parts_of(by_node, 3)[::-1]).astype(BF)
+        copies.append(pltpu.make_async_copy(vertices.at[member], vertex_out.at[member], sems.at[1, member]))
+        copies[-1].start()
+    for copy in copies:
+        copy.wait()
+
+
+def call(kernel, outs, ins, scratch=(), out_spec=VMEM):
     return pl.pallas_call(
         kernel,
         out_shape=[jax.ShapeDtypeStruct(shape, kind) for shape, kind in outs],
-        in_specs=[SMEM] * place + [VMEM] * count,
-        out_specs=[VMEM] * len(outs),
-        scratch_shapes=[pltpu.VMEM(shape, kind) for shape, kind in scratch],
+        in_specs=ins,
+        out_specs=[out_spec] * len(outs),
+        scratch_shapes=[pltpu.VMEM(*spec) if isinstance(spec, tuple) else spec for spec in scratch],
         compiler_params=PARAMS,
     )
 
@@ -263,7 +310,13 @@
     near_pairs = [(i, i ^ 1) for i in range(shards)]
     far_pairs = [(i, (i + 1) % shards if i % 2 else (i - 1) % shards) for i in range(shards)]
 
-    near, far = call(functools.partial(pack_kernel, node_total), [(sent, BF)] * 2, 2)(place, latent, mesh_links)
+    dma = pltpu.SemaphoreType.DMA
+
+    in_hbm = functools.partial(pltpu.with_memory_space_constraint, memory_space=pltpu.HBM)
+
+    near, far = call(
+        functools.partial(pack_kernel, node_total), [(sent, BF)] * 2, [SMEM, HBM, HBM], [(mesh_links.shape, jnp.int32), dma((1 + 2 * members,))]
+    )(place, in_hbm(latent), in_hbm(mesh_links))
     far = lax.ppermute(far, "node", far_pairs)
     near = lax.ppermute(near, "node", near_pairs)
     state, normed_own, normed_next, counts_own = call(
@@ -274,13 +327,23 @@
             ((members, rows, depth), BF),
             ((rows, wide), BF),
         ],
-        7,
-        [((members, wide, depth), BF), ((members, rows + halo, depth), BF)],
-    )(place, latent, mesh_links, near, noise_draw, w_cond, w_in, w_out)
-    decoded, send = call(
-        functools.partial(far_kernel, node_total, groups),
-        [((channels, members * rows), F32), ((groups, channels, members * rows), BF)],
-        13,
+        [SMEM, VMEM] + [HBM] * 6,
+        [
+            ((members, wide, depth), BF),
+            ((members, rows + halo, depth), BF),
+            (mesh_links.shape, jnp.int32),
+            (noise_draw.shape, F32),
+            (w_cond.shape, F32),
+            (latent.shape, BF),
+            (w_in.shape[1:], BF),
+            (w_out.shape[1:], BF),
+            dma((6,)),
+        ],
+    )(place, near, *map(in_hbm, (mesh_links, noise_draw, w_cond, latent, w_in, w_out)))
+    decoded, rounded = call(
+        functools.partial(far_kernel, node_total),
+        [((channels, members * rows), F32), ((channels, members * rows), BF)],
+        [SMEM] + [VMEM] * 13,
         [
             ((members, padded(2 * halo), depth), BF),
             ((members, halo, depth), BF),
@@ -292,20 +355,28 @@
         place, latent, mesh_links, far, noise_draw, w_cond, w_in, w_out, dec_gain.reshape(1, depth), w_dec,
         state, normed_own, normed_next, counts_own,
     )
-    others = lax.all_to_all(send, "member", split_axis=0, concat_axis=0, tiled=True)
+    partner = lax.ppermute(rounded, "member", [(i, i ^ 1) for i in range(groups)])
     weight = location_loss_factor.reshape(1, points)
     incidence, base = call(
         functools.partial(grid_kernel, ensemble),
         [((rows, points), BF), ((members, channels, points), F32)],
-        5,
+        [SMEM] + [VMEM] * 5,
     )(place, decoded, prior_field, target, target_vertex_map.reshape(1, points), weight)
-    prediction_sensitivity, vertex_attribute_sensitivity = call(
+    partner, base = lax.optimization_barrier((partner, base))
+    (stacked,) = call(
+        stack_kernel, [((groups // 2, channels, 2 * members * rows), BF)], [VMEM] * 2
+    )(rounded, partner)
+    others = lax.all_to_all(
+        stacked, "member", split_axis=0, concat_axis=0, tiled=True,
+        axis_index_groups=[list(range(half, groups, 2)) for half in range(2)],
+    )
+    return call(
         functools.partial(score_kernel, ensemble),
         [((members, channels, points), BF), ((members, rows, depth), BF)],
-        6,
-        place=False,
-    )(decoded, others, incidence, base, weight, w_dec)
-    return prediction_sensitivity, vertex_attribute_sensitivity
+        [VMEM] * 6,
+        [((members, channels, points), BF), ((members, rows, depth), BF), dma((2, members))],
+        HBM,
+    )(rounded, others, incidence, base, weight, w_dec)
 
 
 def solution(mesh):

time: 63.2 us -> 55.3 us (0.87)
  the two profiles are of different devices: /device:TPU:120 before, /device:TPU:57 now
where the time goes in v2:
time: 55.3 us; the launch traced here: 55 us
  starting transfers between devices  16.6 us (30%)
  Pallas kernels  16.2 us (29%)
  blocking collectives  14.9 us (27%)
  waiting for transfers between devices  5.12 us (9%)
  local copies, waits for them, and re-layouts  1.16 us (2%)
  between operations  0.89 us (2%)
    all_to_all x1, blocking collectives, per_device(): lax.all_to_all(stacked, 'member', split_axis=0, concat_axis=0, tiled=True...  14.9 us
    ppermute x1, starting transfers between devices, per_device(): lax.ppermute(rounded, 'member', [(i, i ^ 1) for i in range(groups)])  10.6 us
    pallas_call x1, Pallas kernels, per_device(): call(functools.partial(far_kernel, node_total), [((channels, members * ro...  4.95 us
    pallas_call x1, Pallas kernels, per_device(): call(functools.partial(near_kernel, node_total), [((members, rows, depth)...  4.38 us
    ppermute x1, waiting for transfers between devices, per_device(): far = lax.ppermute(far, 'node', far_pairs)  3.87 us
    pallas_call x1, Pallas kernels, per_device(): call(functools.partial(score_kernel, ensemble), [((members, channels, poi...  3.64 us
    ppermute x1, starting transfers between devices, per_device(): far = lax.ppermute(far, 'node', far_pairs)  3.37 us
    ppermute x1, starting transfers between devices, per_device(): near = lax.ppermute(near, 'node', near_pairs)  2.58 us
  transfers between devices with their start and end apart: 3, of which 2 were waited for; matrix products, arithmetic and copies ran while one was open for 0% of the time, Pallas kernels for 10%

profile of v2, /device:TPU:57, one launch (start us, length us, event | category | flops | bytes accessed | tf_op | source)
XLA Modules:
  0.0 55.0 jit_solution(13604664709736249112)
XLA Ops:
  0.6 0.1 pad_add_fusion.place
  0.7 1.8 %shard_map.131 = (bf16[400,512]{1,0:T(8,128)(2,1)S(1)}, bf16[400,512]{1,0:T(8,128)(2,1)S(1)}) custom-call(s32[2]{0:T(128)S(1)} %pad_add_fusion.place, bf16[2,256,512]{2,1,0:T(8,128)(2,1)} %latent.3, s32[6,256]{1,0:T(8,128)} %links.1), custom_call_target="tpu_custom_call" | custom-call | tf_op jit(solution)/shard_map/pallas_call | solution.py:317
  2.5 2.6 %collective-permute-start.1 = (bf16[400,512]{1,0:T(8,128)(2,1)S(1)}, bf16[400,512]{1,0:T(8,128)(2,1)S(1)}, u32[]{:S(2)}, u32[]{:S(2)}) collective-permute-start(bf16[400,512]{1,0:T(8,128)(2,1)S(1)} %get-tuple-element.15), channel_id=1, source_target_pairs={{0,1},{1,0},{2,3},{3,2},{4,5},{5,4},{6,7},{7,6},{8,9},{9,8},{10,11... | collective-permute-start | bytes 1228808 | tf_op jit(solution)/shard_map/ppermute | solution.py:321
  5.1 0.0 copy-start
  5.1 0.0 copy-start.1
  5.2 0.0 copy-start.2
  5.2 0.0 copy-start.3
  5.2 0.0 copy-start.4
  5.2 0.0 copy-start.7
  5.2 0.0 copy-start.10
  5.2 0.0 copy-start.11
  5.2 3.4 %collective-permute-start = (bf16[400,512]{1,0:T(8,128)(2,1)S(1)}, bf16[400,512]{1,0:T(8,128)(2,1)S(1)}, u32[]{:S(2)}, u32[]{:S(2)}) collective-permute-start(bf16[400,512]{1,0:T(8,128)(2,1)S(1)} %get-tuple-element.14), channel_id=1, source_target_pairs={{0,63},{1,2},{2,1},{3,4},{4,3},{5,6},{6,5},{7,8},{8,7},{9,10},{10,... | collective-permute-start | bytes 1228808 | tf_op jit(solution)/shard_map/ppermute | solution.py:320
  8.6 0.0 collective-permute-done.1.near
  8.6 4.4 %shard_map.132 = (f32[2,256,512]{2,1,0:T(8,128)S(1)}, bf16[2,256,512]{2,1,0:T(8,128)(2,1)S(1)}, bf16[2,256,512]{2,1,0:T(8,128)(2,1)S(1)}, bf16[256,512]{1,0:T(8,128)(2,1)S(1)}) custom-call(s32[2]{0:T(128)S(1)} %pad_add_fusion.place, bf16[400,512]{1,0:T(8,128)(2,1)S(1)} %collective-permute-done.1.near, s32[6,256]{1,0:T(8,128)} %links.1, f32[2,32]{1,0:T(2,128)} %noise.1, ...), custom_call_target="tpu_custom_call" | custom-call | tf_op jit(solution)/shard_map/pallas_call | solution.py:322
  13.0 3.9 %collective-permute-done.far = bf16[400,512]{1,0:T(8,128)(2,1)S(1)} collective-permute-done((bf16[400,512]{1,0:T(8,128)(2,1)S(1)}, bf16[400,512]{1,0:T(8,128)(2,1)S(1)}, u32[]{:S(2)}, u32[]{:S(2)}) %collective-permute-start) | collective-permute-done | bytes 409632 | tf_op jit(solution)/shard_map/ppermute | solution.py:320
  16.9 0.0 copy-done
  16.9 0.0 copy-done.1
  16.9 0.0 copy-done.2
  16.9 0.0 copy-done.3
  16.9 0.0 copy-done.4
  16.9 0.0 copy-start.5
  16.9 0.0 copy-start.6
  17.0 0.0 copy-start.8
  17.0 0.0 copy-start.9
  17.0 5.0 %shard_map.133 = (f32[83,512]{1,0:T(8,128)S(1)}, bf16[83,512]{1,0:T(8,128)(2,1)S(1)}) custom-call(s32[2]{0:T(128)S(1)} %pad_add_fusion.place, bf16[2,256,512]{2,1,0:T(8,128)(2,1)S(1)} %copy-done.1, s32[6,256]{1,0:T(8,128)S(1)} %copy-done.7, bf16[400,512]{1,0:T(8,128)(2,1)S(1)} %collective-permute-done.far, f32[2,32]{1,0:T(2,128)S(1)} %copy-done.10, ...), custom_call_target="tpu_custom_call" | custom-call | tf_op jit(solution)/shard_map/pallas_call | solution.py:343
  21.9 10.6 %collective-permute-start.2 = (bf16[83,512]{1,0:T(8,128)(2,1)S(1)}, bf16[83,512]{1,0:T(8,128)(2,1)S(1)}, u32[]{:S(2)}, u32[]{:S(2)}) collective-permute-start(bf16[83,512]{1,0:T(8,128)(2,1)S(1)} %get-tuple-element.20.mine.rounded), channel_id=1, source_target_pairs={{0,64},{64,0},{128,192},{192,128},{256,320},{320,256},{384,448},{4... | collective-permute-start | bytes 254984 | tf_op jit(solution)/shard_map/ppermute | solution.py:358
  32.6 1.4 %shard_map.134 = (bf16[256,1024]{1,0:T(8,128)(2,1)S(1)}, f32[2,83,1024]{2,1,0:T(8,128)S(1)}) custom-call(s32[2]{0:T(128)S(1)} %pad_add_fusion.place, f32[83,512]{1,0:T(8,128)S(1)} %get-tuple-element.21.decoded, bf16[83,1024]{1,0:T(8,128)(2,1)S(1)} %copy-done.5, bf16[83,1024]{1,0:T(8,128)(2,1)S(1)} %copy-done.6, s32[1,1024]{1,0:T(1,128)S(1)} %bitcast.7, ...), custom_call_target="tpu_custom_call" | custom-call | tf_op jit(solution)/shard_map/pallas_call | solution.py:360
  34.0 1.2 %collective-permute-done.2.partner = bf16[83,512]{1,0:T(8,128)(2,1)S(1)} collective-permute-done((bf16[83,512]{1,0:T(8,128)(2,1)S(1)}, bf16[83,512]{1,0:T(8,128)(2,1)S(1)}, u32[]{:S(2)}, u32[]{:S(2)}) %collective-permute-start.2) | collective-permute-done | bytes 85024 | tf_op jit(solution)/shard_map/ppermute | solution.py:358
  35.3 0.1 shard_map.135
  35.3 14.9 %all_to_all.5.others = bf16[4,83,1024]{2,1,0:T(8,128)(2,1)S(1)} all-to-all(bf16[4,83,1024]{2,1,0:T(8,128)(2,1)S(1)} %shard_map.135), channel_id=1, replica_groups={{0,128,256,384},{64,192,320,448},{1,129,257,385},{65,193,321,449},{2,13..., dimensions={0} | all-to-all | bytes 1359872 | tf_op jit(solution)/shard_map/all_to_all | solution.py:369
  50.3 3.6 %shard_map.136 = (bf16[2,83,1024]{2,1,0:T(8,128)(2,1)S(1)}, bf16[2,256,512]{2,1,0:T(8,128)(2,1)}) custom-call(bf16[83,512]{1,0:T(8,128)(2,1)S(1)} %get-tuple-element.20.mine.rounded, bf16[4,83,1024]{2,1,0:T(8,128)(2,1)S(1)} %all_to_all.5.others, bf16[256,1024]{1,0:T(8,128)(2,1)S(1)} %get-tuple-element.24.incidence, ...), custom_call_target="tpu_custom_call" | custom-call | tf_op jit(solution)/shard_map/pallas_call | solution.py:373
  53.9 1.1 %copy.14 = bf16[2,83,1024]{2,0,1:T(2,128)(2,1)} copy(bf16[2,83,1024]{2,1,0:T(8,128)(2,1)S(1)} %get-tuple-element.26) | data formatting | bytes 679936 | tf_op jit(solution)/shard_map/pallas_call | solution.py:373
  (7 shorter events, 0.0 us)
Async XLA Ops:
  2.5 6.1 %collective-permute-start.1 = (bf16[400,512]{1,0:T(8,128)(2,1)S(1)}, bf16[400,512]{1,0:T(8,128)(2,1)S(1)}, u32[]{:S(2)}, u32[]{:S(2)}) collective-permute-start(bf16[400,512]{1,0:T(8,128)(2,1)S(1)} %get-tuple-element.15), channel_id=1, source_target_pairs={{0,1},{1,0},{2,3},{3,2},{4,5},{5,4},{6,7},{7,6},{8,9},{9,8},{10,11... | collective-permute-start | bytes 1228808 | tf_op jit(solution)/shard_map/ppermute | solution.py:321
  5.1 11.7 %copy-start = (bf16[2,1024,512]{2,1,0:T(8,128)(2,1)S(1)}, bf16[2,1024,512]{2,1,0:T(8,128)(2,1)}, u32[]{:S(2)}) copy-start(bf16[2,1024,512]{2,1,0:T(8,128)(2,1)} %w_in.1) | copy-start | bytes 6291460
  5.1 11.7 %copy-start.1 = (bf16[2,256,512]{2,1,0:T(8,128)(2,1)S(1)}, bf16[2,256,512]{2,1,0:T(8,128)(2,1)}, u32[]{:S(2)}) copy-start(bf16[2,256,512]{2,1,0:T(8,128)(2,1)} %latent.3) | copy-start | bytes 1572868
  5.2 11.7 %copy-start.2 = (bf16[2,512,512]{2,1,0:T(8,128)(2,1)S(1)}, bf16[2,512,512]{2,1,0:T(8,128)(2,1)}, u32[]{:S(2)}) copy-start(bf16[2,512,512]{2,1,0:T(8,128)(2,1)} %w_out.1) | copy-start | bytes 3145732
  5.2 11.7 %copy-start.3 = (f32[2,32,512]{2,1,0:T(8,128)S(1)}, f32[2,32,512]{2,1,0:T(8,128)}, u32[]{:S(2)}) copy-start(f32[2,32,512]{2,1,0:T(8,128)} %w_cond.1) | copy-start | bytes 393220
  5.2 11.7 %copy-start.4 = (bf16[83,512]{1,0:T(8,128)(2,1)S(1)}, bf16[83,512]{1,0:T(8,128)(2,1)}, u32[]{:S(2)}) copy-start(bf16[83,512]{1,0:T(8,128)(2,1)} %w_dec.3) | copy-start | bytes 254980
  5.2 11.7 %copy-start.7 = (s32[6,256]{1,0:T(8,128)S(1)}, s32[6,256]{1,0:T(8,128)}, u32[]{:S(2)}) copy-start(s32[6,256]{1,0:T(8,128)} %links.1) | copy-start | bytes 18436
  5.2 11.7 %copy-start.10 = (f32[2,32]{1,0:T(2,128)S(1)}, f32[2,32]{1,0:T(2,128)}, u32[]{:S(2)}) copy-start(f32[2,32]{1,0:T(2,128)} %noise.1) | copy-start | bytes 772
  5.2 11.7 %copy-start.11 = (f32[512]{0:T(512)S(1)}, f32[512]{0:T(512)}, u32[]{:S(2)}) copy-start(f32[512]{0:T(512)} %param.18) | copy-start | bytes 6148
  5.2 11.6 %collective-permute-start = (bf16[400,512]{1,0:T(8,128)(2,1)S(1)}, bf16[400,512]{1,0:T(8,128)(2,1)S(1)}, u32[]{:S(2)}, u32[]{:S(2)}) collective-permute-start(bf16[400,512]{1,0:T(8,128)(2,1)S(1)} %get-tuple-element.14), channel_id=1, source_target_pairs={{0,63},{1,2},{2,1},{3,4},{4,3},{5,6},{6,5},{7,8},{8,7},{9,10},{10,... | collective-permute-start | bytes 1228808 | tf_op jit(solution)/shard_map/ppermute | solution.py:320
  16.9 15.7 %copy-start.5 = (bf16[83,1024]{1,0:T(8,128)(2,1)S(1)}, bf16[83,1024]{1,0:T(8,128)(2,1)}, u32[]{:S(2)}) copy-start(bf16[83,1024]{1,0:T(8,128)(2,1)} %prior.1) | copy-start | bytes 509956
  16.9 15.7 %copy-start.6 = (bf16[83,1024]{1,0:T(8,128)(2,1)S(1)}, bf16[83,1024]{1,0:T(8,128)(2,1)}, u32[]{:S(2)}) copy-start(bf16[83,1024]{1,0:T(8,128)(2,1)} %target.1) | copy-start | bytes 509956
  17.0 15.7 %copy-start.8 = (f32[1024]{0:T(1024)S(1)}, f32[1024]{0:T(1024)}, u32[]{:S(2)}) copy-start(f32[1024]{0:T(1024)} %param.23) | copy-start | bytes 12292
  17.0 15.7 %copy-start.9 = (s32[1024]{0:T(1024)S(1)}, s32[1024]{0:T(1024)}, u32[]{:S(2)}) copy-start(s32[1024]{0:T(1024)} %param.20) | copy-start | bytes 12292
  21.9 13.3 %collective-permute-start.2 = (bf16[83,512]{1,0:T(8,128)(2,1)S(1)}, bf16[83,512]{1,0:T(8,128)(2,1)S(1)}, u32[]{:S(2)}, u32[]{:S(2)}) collective-permute-start(bf16[83,512]{1,0:T(8,128)(2,1)S(1)} %get-tuple-element.20.mine.rounded), channel_id=1, source_target_pairs={{0,64},{64,0},{128,192},{192,128},{256,320},{320,256},{384,448},{4... | collective-permute-start | bytes 254984 | tf_op jit(solution)/shard_map/ppermute | solution.py:358

commit v3 on v2

v3 whole, which is shorter than its diff:
```python
import functools

import jax
import jax.numpy as jnp
from jax import lax
from jax.experimental import pallas as pl
from jax.experimental.pallas import tpu as pltpu
from jax.sharding import PartitionSpec as P

WIN = 96
NORM_EPS = 1e-06
DIST_EPS = 1e-06

LONG = 10**11

BF = jnp.bfloat16
F32 = jnp.float32
VMEM = pl.BlockSpec(memory_space=pltpu.VMEM)
HBM = pl.BlockSpec(memory_space=pltpu.HBM)
PARAMS = pltpu.CompilerParams(vmem_limit_bytes=40 * 2**20)


def dot(lhs, rhs):
    return jnp.dot(lhs, rhs, preferred_element_type=F32)


def dot_nt(lhs, rhs):
    return lax.dot_general(lhs, rhs, (((1,), (1,)), ((), ())), preferred_element_type=F32)


def norm(values, scaling):
    inverse = lax.rsqrt(jnp.mean(values * values, axis=-1, keepdims=True) + NORM_EPS)
    return (values * inverse * scaling).astype(BF)


def silu(values):
    half = 0.5 * values
    return half + half * jnp.tanh(half)


def parts_of(values, count):
    parts = []
    for _ in range(count):
        part = values.astype(BF)
        parts.append(part)
        values = values - part.astype(F32)
    return parts


def padded(rows):
    return -(-rows // 256) * 256


def gains(noise_ref, w_cond_ref, layer):
    return 1.0 + jnp.dot(
        noise_ref[...], w_cond_ref[layer], precision=lax.Precision.HIGHEST, preferred_element_type=F32
    )


def link_offsets(links, first, node_total):
    own = first + lax.broadcasted_iota(jnp.int32, links.shape, 1)
    away = links - own
    away = jnp.where(away > node_total // 2, away - node_total, away)
    away = jnp.where(away < -(node_total // 2), away + node_total, away)
    return away.astype(F32)


def count_matrix(offsets, width):
    link_count, rows = offsets.shape
    places = offsets + (WIN + lax.broadcasted_iota(jnp.int32, offsets.shape, 1)).astype(F32)
    places = jnp.concatenate([places, jnp.full((128 - link_count, rows), -1.0, F32)], axis=0).T
    columns = lax.broadcasted_iota(jnp.int32, (rows, width), 1).astype(F32)
    total = jnp.zeros((rows, width), F32)
    for slot in range(link_count):
        total = total + jnp.where(columns == places[:, slot : slot + 1], 1.0, 0.0)
    return total.astype(BF)


def layer(values, normed, windows, counts, w_in, w_out, link_count):
    rows = values.shape[0] // len(windows)
    sums = [dot(counts, window)[:rows] for window in windows]
    neighbours = (jnp.concatenate(sums, axis=0) * (1.0 / link_count)).astype(BF)
    depth = normed.shape[1]
    preact = dot(normed, w_in[:depth]) + dot(neighbours, w_in[depth:])
    return values + dot(silu(preact).astype(BF), w_out)


def rows_of(array, start, count):
    return jnp.concatenate([array[member, start : start + count] for member in range(array.shape[0])], axis=0)


def position(shards, rows):
    shard = lax.axis_index("node")
    return lax.rem(shard, 2), shard * rows, shards * rows


def fetch_all(pairs, sems):
    fetches = [pltpu.make_async_copy(there, here, sems.at[at]) for at, (there, here) in enumerate(pairs)]
    for fetch in fetches:
        fetch.start()
    return fetches


def pack_kernel(shards, latent, links_in, near, far, links, sems):
    halo = 2 * WIN
    members, rows, _ = latent.shape
    odd, first, node_total = position(shards, rows)
    pairs = [(links_in, links)]
    for send, start in ((near, (1 - odd) * (rows - halo)), (far, odd * (rows - halo))):
        start = pl.multiple_of(start, 64)
        for member in range(members):
            pairs.append((latent.at[member, pl.ds(start, halo)], send.at[pl.ds(member * halo, halo)]))
    fetches = fetch_all(pairs, sems)
    fetches[0].wait()
    offsets = link_offsets(links[...], first, node_total).astype(BF)
    tail = members * halo
    for send in (near, far):
        send[tail:] = jnp.zeros((send.shape[0] - tail, send.shape[1]), BF)
        send[tail : tail + offsets.shape[0], : offsets.shape[1]] = offsets
    for fetch in fetches[1:]:
        fetch.wait()


def received_offsets(received, tail, link_count, rows):
    return received[tail : tail + 16, :rows].astype(F32)[:link_count]


def near_kernel(
    shards, near, links_in, noise_in, w_cond_in, latent_in, vertex_in, w_in_in, w_out_in,
    state_out, normed_own_out, normed_next_out, counts_out, scaling_out, incidence_out, window, inputs,
    links, noise, w_cond, latent, vertex, w_in, w_out, sems
):
    fetches = fetch_all(
        (
            (links_in, links),
            (noise_in, noise),
            (w_cond_in, w_cond),
            (latent_in, latent),
            (vertex_in, vertex),
            (w_in_in.at[0], w_in),
            (w_out_in.at[0], w_out),
        ),
        sems,
    )
    members, rows, _ = latent.shape
    odd, first, node_total = position(shards, rows)
    link_count = links.shape[0]
    halo = 2 * WIN
    own_at = pl.multiple_of(odd * halo, 64)
    near_at = pl.multiple_of((1 - odd) * rows, 64)
    fetches[0].wait()
    own_offsets = link_offsets(links[...], first, node_total)
    near_offsets = received_offsets(near, members * halo, link_count, rows)
    lane = lax.broadcasted_iota(jnp.int32, own_offsets.shape, 1)
    mine = jnp.logical_and(lane >= (1 - odd) * WIN, lane < rows - odd * WIN)
    mixed = jnp.where(mine, own_offsets, near_offsets)
    mixed = pltpu.roll(mixed, rows - WIN - odd * (rows - 2 * WIN), 1)
    counts = count_matrix(mixed, window.shape[1])
    counts_out[...] = count_matrix(own_offsets, window.shape[1])
    for fetch in fetches[1:5]:
        fetch.wait()
    scaling = gains(noise, w_cond, 0)
    next_scaling = gains(noise, w_cond, 1)
    scaling_out[0] = scaling
    scaling_out[1] = next_scaling
    for member in range(members):
        scale = scaling[member : member + 1]
        own = latent[member]
        edge = near[member * halo : (member + 1) * halo]
        inputs[member, pl.ds(own_at, rows)] = own
        inputs[member, pl.ds(near_at, halo)] = edge
        normed_own = norm(own.astype(F32), scale)
        normed_own_out[member] = normed_own
        window[member, rows + halo :] = jnp.zeros((window.shape[1] - rows - halo, window.shape[2]), BF)
        window[member, pl.ds(own_at, rows)] = normed_own
        window[member, pl.ds(near_at, halo)] = norm(edge.astype(F32), scale)
    for fetch in fetches[5:]:
        fetch.wait()
    values = layer(
        rows_of(inputs, WIN, rows).astype(F32), rows_of(window, WIN, rows), [window[m] for m in range(members)],
        counts, w_in[...], w_out[...], link_count,
    )
    for member in range(members):
        own = values[member * rows : (member + 1) * rows]
        state_out[member] = own
        normed_next_out[member] = norm(own, next_scaling[member : member + 1])
    ids = first + lax.broadcasted_iota(jnp.int32, incidence_out.shape, 0)
    incidence_out[...] = jnp.where(ids == vertex[...], 1.0, 0.0).astype(BF)


def far_kernel(
    shards, latent, links, far, scaling, w_in, w_out, dec_gain, w_dec,
    state_in, normed_own, normed_next, counts_own, decoded_out, rounded_out,
    window, inputs, state, window_next,
):
    members, rows, _ = latent.shape
    odd, first, node_total = position(shards, rows)
    even = 1 - odd
    link_count = links.shape[0]
    halo = 2 * WIN
    filled = rows + halo
    own_offsets = link_offsets(links[...], first, node_total)
    far_offsets = received_offsets(far, members * halo, link_count, rows)
    lane = lax.broadcasted_iota(jnp.int32, own_offsets.shape, 1)
    mine = jnp.logical_or(
        jnp.logical_and(odd == 0, lane < WIN), jnp.logical_and(odd == 1, lane >= rows - WIN)
    )
    counts = count_matrix(pltpu.roll(jnp.where(mine, own_offsets, far_offsets), WIN, 1), window.shape[1])
    far_at = pl.multiple_of(odd * rows, 64)
    near_at = pl.multiple_of(even * halo, 64)
    for member in range(members):
        window[member, 2 * halo :] = jnp.zeros((window.shape[1] - 2 * halo, window.shape[2]), BF)
        window_next[member, filled:] = jnp.zeros((window_next.shape[1] - filled, window_next.shape[2]), BF)
        edge = far[member * halo : (member + 1) * halo]
        window[member, pl.ds(pl.multiple_of(odd * halo, 64), halo)] = norm(
            edge.astype(F32), scaling[0, member : member + 1]
        )
        window[member, pl.ds(pl.multiple_of(even * halo, 64), halo)] = normed_own[
            member, pl.ds(pl.multiple_of(odd * (rows - halo), 64), halo)
        ]
        inputs[member, pl.ds(pl.multiple_of(odd * WIN, 32), WIN)] = far[
            pl.ds(pl.multiple_of(member * halo + even * WIN, 32), WIN)
        ]
        inputs[member, pl.ds(pl.multiple_of(even * WIN, 32), WIN)] = latent[
            member, pl.ds(pl.multiple_of(odd * (rows - WIN), 32), WIN)
        ]
        state[member, pl.ds(near_at, rows)] = state_in[member]
        window_next[member, pl.ds(near_at, rows)] = normed_next[member]
    values = layer(
        rows_of(inputs, 0, halo).astype(F32), rows_of(window, WIN, halo), [window[m] for m in range(members)],
        counts, w_in[0], w_out[0], link_count,
    )
    for member in range(members):
        own = values[member * halo : (member + 1) * halo]
        state[member, pl.ds(far_at, halo)] = own
        window_next[member, pl.ds(far_at, halo)] = norm(own, scaling[1, member : member + 1])
    values = layer(
        rows_of(state, WIN, rows), rows_of(window_next, WIN, rows), [window_next[m] for m in range(members)],
        counts_own[...], w_in[1], w_out[1], link_count,
    )
    decoded = dot_nt(w_dec[...], norm(values, dec_gain[...]))
    decoded_out[...] = decoded
    rounded_out[...] = decoded.astype(BF)


def stack_kernel(mine, partner, out):
    wide = mine.shape[1]
    for copy in range(out.shape[0]):
        out[copy, :, :wide] = mine[...]
        out[copy, :, wide:] = partner[...]


def at_grid(parts, incidence):
    channels = parts[0].shape[0]
    fill = -channels % 16
    tail = jnp.zeros((fill, parts[0].shape[1]), BF)
    stacked = jnp.concatenate([piece for part in parts for piece in (part, tail)], axis=0)
    found = dot(stacked, incidence[...])
    step = channels + fill
    return [found[at * step : at * step + channels] for at in range(len(parts))]


def grid_kernel(ensemble, decoded, prior, target, weight, incidence, base_out):
    members = base_out.shape[0]
    nodes = incidence.shape[0]
    own = [part for m in range(members) for part in parts_of(decoded[:, m * nodes : (m + 1) * nodes], 3)]
    at_points = at_grid(own, incidence)
    before = prior[...].astype(F32)
    truth = target[...].astype(F32)
    for member in range(members):
        high, middle, low = at_points[3 * member : 3 * member + 3]
        missed = (before + (low + middle + high)).astype(BF).astype(F32) - truth
        reached = lax.rsqrt(jnp.sum(missed * missed, axis=0, keepdims=True) + DIST_EPS)
        base_out[member] = missed * (reached * weight[...] * (1.0 / ensemble))


def pull_sums(rounded, others, member, members):
    nodes = rounded.shape[1] // members
    step = 128
    pulls = []
    for start in range(member * nodes, (member + 1) * nodes, step):
        anchor = rounded[:, start : start + step].astype(F32)
        total = jnp.zeros_like(anchor)
        for group in range(others.shape[0]):
            for at in range(start % nodes, others.shape[2], nodes):
                offset = anchor - others[group, :, at : at + step].astype(F32)
                near = jnp.sum(offset * offset, axis=0, keepdims=True) + DIST_EPS
                total = total + offset * lax.rsqrt(near)
        pulls.append(total)
    return jnp.concatenate(pulls, axis=1)


def score_kernel(
    ensemble, rounded, others, incidence, base, weight, w_dec, grad_out, vertex_out, grads, vertices, sems
):
    members, channels, _ = base.shape
    nodes = incidence.shape[0]
    factor = weight[...] * (1.0 / (ensemble * (ensemble - 1)))
    copies = []
    pull = [part for m in range(members) for part in parts_of(pull_sums(rounded, others, m, members), 2)]
    at_points = at_grid(pull, incidence)
    for member in range(members):
        high, low = at_points[2 * member : 2 * member + 2]
        grads[member] = (base[member] - factor * (low + high)).astype(BF)
        copies.append(pltpu.make_async_copy(grads.at[member], grad_out.at[member], sems.at[0, member]))
        copies[-1].start()
    for member in range(members):
        high, middle, low = parts_of(dot_nt(incidence[...], grads[member]), 3)
        vertices[member] = (dot(low, w_dec[...]) + dot(middle, w_dec[...]) + dot(high, w_dec[...])).astype(BF)
        copies.append(pltpu.make_async_copy(vertices.at[member], vertex_out.at[member], sems.at[1, member]))
        copies[-1].start()
    for copy in copies:
        copy.wait()


def call(kernel, outs, ins, scratch=(), out_spec=VMEM, weight=0):
    return pl.pallas_call(
        kernel,
        out_shape=[jax.ShapeDtypeStruct(shape, kind) for shape, kind in outs],
        in_specs=ins,
        out_specs=[out_spec] * len(outs),
        scratch_shapes=[pltpu.VMEM(*spec) if isinstance(spec, tuple) else spec for spec in scratch],
        compiler_params=PARAMS,
        cost_estimate=pl.CostEstimate(flops=weight, bytes_accessed=0, transcendentals=0) if weight else None,
    )


def per_device(
    latent, noise_draw, mesh_links, w_cond, w_in, w_out, dec_gain, w_dec,
    target_vertex_map, prior_field, target, location_loss_factor,
):
    members, rows, depth = latent.shape
    channels, points = prior_field.shape
    shards = lax.axis_size("node")
    groups = lax.axis_size("member")
    ensemble = members * groups
    halo = 2 * WIN
    wide = padded(rows + halo)
    sent = (members * halo + 16, depth)
    near_pairs = [(i, i ^ 1) for i in range(shards)]
    far_pairs = [(i, (i + 1) % shards if i % 2 else (i - 1) % shards) for i in range(shards)]

    dma = pltpu.SemaphoreType.DMA

    in_hbm = functools.partial(pltpu.with_memory_space_constraint, memory_space=pltpu.HBM)

    vertex = target_vertex_map.reshape(1, points)
    near, far = call(
        functools.partial(pack_kernel, shards), [(sent, BF)] * 2, [HBM, HBM], [(mesh_links.shape, jnp.int32), dma((1 + 2 * members,))]
    )(in_hbm(latent), in_hbm(mesh_links))
    far = lax.ppermute(far, "node", far_pairs)
    near = lax.ppermute(near, "node", near_pairs)
    state, normed_own, normed_next, counts_own, scaling, incidence = call(
        functools.partial(near_kernel, shards),
        [
            ((members, rows, depth), F32),
            ((members, rows, depth), BF),
            ((members, rows, depth), BF),
            ((rows, wide), BF),
            ((w_cond.shape[0], members, depth), F32),
            ((rows, points), BF),
        ],
        [VMEM] + [HBM] * 7,
        [
            ((members, wide, depth), BF),
            ((members, rows + halo, depth), BF),
            (mesh_links.shape, jnp.int32),
            (noise_draw.shape, F32),
            (w_cond.shape, F32),
            (latent.shape, BF),
            ((1, points), jnp.int32),
            (w_in.shape[1:], BF),
            (w_out.shape[1:], BF),
            dma((7,)),
        ],
    )(near, *map(in_hbm, (mesh_links, noise_draw, w_cond, latent, vertex, w_in, w_out)))
    decoded, rounded = call(
        functools.partial(far_kernel, shards),
        [((channels, members * rows), F32), ((channels, members * rows), BF)],
        [VMEM] * 12,
        [
            ((members, padded(2 * halo), depth), BF),
            ((members, halo, depth), BF),
            ((members, rows + halo, depth), F32),
            ((members, wide, depth), BF),
        ],
    )(
        latent, mesh_links, far, scaling, w_in, w_out, dec_gain.reshape(1, depth), w_dec,
        state, normed_own, normed_next, counts_own,
    )
    partner = lax.ppermute(rounded, "member", [(i, i ^ 1) for i in range(groups)])
    weight = location_loss_factor.reshape(1, points)
    (base,) = call(
        functools.partial(grid_kernel, ensemble), [((members, channels, points), F32)], [VMEM] * 5
    )(decoded, prior_field, target, weight, incidence)
    partner, base = lax.optimization_barrier((partner, base))
    sides = 2
    (stacked,) = call(
        stack_kernel, [((groups // sides, channels, sides * members * rows), BF)], [VMEM] * 2
    )(rounded, partner)
    others = lax.all_to_all(
        stacked, "member", split_axis=0, concat_axis=0, tiled=True,
        axis_index_groups=[list(range(side, groups, sides)) for side in range(sides)],
    )
    return call(
        functools.partial(score_kernel, ensemble),
        [((members, channels, points), BF), ((members, rows, depth), BF)],
        [VMEM] * 6,
        [((members, channels, points), BF), ((members, rows, depth), BF), dma((2, members))],
        HBM,
    )(rounded, others, incidence, base, weight, w_dec)


def solution(mesh):
    in_specs = (
        P("member", "node", None),
        P("member", None),
        P(None, "node"),
        P(),
        P(),
        P(),
        P(),
        P(),
        P("node"),
        P(None, "node"),
        P(None, "node"),
        P("node"),
    )
    out_specs = (P("member", None, "node"), P("member", "node", None))
    return jax.shard_map(
        per_device, mesh=mesh, in_specs=in_specs, out_specs=out_specs, check_vma=False
    )
```

time: 55.3 us -> 52.8 us (0.955)
  Pallas kernels: 16.2 us -> 12.9 us
  waiting for transfers between devices: 5.12 us -> 6.45 us
    pallas_call x5, Pallas kernels: 12.6 us -> 9.3 us  [the longest x1 3.8 us: per_device(): call(functools.partial(near_kernel, shards), [((members, rows, depth), F3...]
    ppermute x1, waiting for transfers between devices: 1.24 us -> 2.07 us  [per_device(): lax.ppermute(rounded, 'member', [(i, i ^ 1) for i in range(groups)])]
  transfers between devices with their start and end apart: 3 -> 3, of which waited for: 2 -> 2; matrix products, arithmetic and copies ran while one was open for 0% -> 0% of each run, Pallas kernels for 10% -> 8%
where the time goes in v3:
time: 52.8 us; the launch traced here: 52.6 us
  starting transfers between devices  16.3 us (31%)
  blocking collectives  15 us (28%)
  Pallas kernels  12.9 us (24%)
  waiting for transfers between devices  6.45 us (12%)
  local copies, waits for them, and re-layouts  1.14 us (2%)
  between operations  0.83 us (2%)
    all_to_all x1, blocking collectives, per_device(): lax.all_to_all(stacked, 'member', split_axis=0, concat_axis=0, tiled=True...  15 us
    ppermute x1, starting transfers between devices, per_device(): lax.ppermute(rounded, 'member', [(i, i ^ 1) for i in range(groups)])  10.6 us
    ppermute x1, waiting for transfers between devices, per_device(): far = lax.ppermute(far, 'node', far_pairs)  4.38 us
    pallas_call x1, Pallas kernels, per_device(): call(functools.partial(near_kernel, shards), [((members, rows, depth), F3...  3.8 us
    pallas_call x1, Pallas kernels, per_device(): call(functools.partial(far_kernel, shards), [((channels, members * rows),...  3.61 us
    pallas_call x1, Pallas kernels, per_device(): call(functools.partial(score_kernel, ensemble), [((members, channels, poi...  3.61 us
    ppermute x1, starting transfers between devices, per_device(): far = lax.ppermute(far, 'node', far_pairs)  3.1 us
    ppermute x1, starting transfers between devices, per_device(): near = lax.ppermute(near, 'node', near_pairs)  2.58 us
  transfers between devices with their start and end apart: 3, of which 2 were waited for; matrix products, arithmetic and copies ran while one was open for 0% of the time, Pallas kernels for 8%

profile of v3, /device:TPU:57, one launch (start us, length us, event | category | flops | bytes accessed | tf_op | source)
XLA Modules:
  0.0 52.6 jit_solution(16889574186507616580)
XLA Ops:
  0.6 1.3 %shard_map.131 = (bf16[400,512]{1,0:T(8,128)(2,1)S(1)}, bf16[400,512]{1,0:T(8,128)(2,1)S(1)}) custom-call(bf16[2,256,512]{2,1,0:T(8,128)(2,1)} %latent.3, s32[6,256]{1,0:T(8,128)} %links.1), custom_call_target="tpu_custom_call" | custom-call | tf_op jit(solution)/shard_map/pallas_call | solution.py:348
  1.9 2.6 %collective-permute-start.1 = (bf16[400,512]{1,0:T(8,128)(2,1)S(1)}, bf16[400,512]{1,0:T(8,128)(2,1)S(1)}, u32[]{:S(2)}, u32[]{:S(2)}) collective-permute-start(bf16[400,512]{1,0:T(8,128)(2,1)S(1)} %get-tuple-element.15), channel_id=1, source_target_pairs={{0,1},{1,0},{2,3},{3,2},{4,5},{5,4},{6,7},{7,6},{8,9},{9,8},{10,11... | collective-permute-start | bytes 1228808 | tf_op jit(solution)/shard_map/ppermute | solution.py:352
  4.5 3.1 %collective-permute-start = (bf16[400,512]{1,0:T(8,128)(2,1)S(1)}, bf16[400,512]{1,0:T(8,128)(2,1)S(1)}, u32[]{:S(2)}, u32[]{:S(2)}) collective-permute-start(bf16[400,512]{1,0:T(8,128)(2,1)S(1)} %get-tuple-element.14), channel_id=1, source_target_pairs={{0,63},{1,2},{2,1},{3,4},{4,3},{5,6},{6,5},{7,8},{8,7},{9,10},{10,... | collective-permute-start | bytes 1228808 | tf_op jit(solution)/shard_map/ppermute | solution.py:351
  7.6 0.0 collective-permute-done.1.near
  7.6 0.0 copy-start
  7.6 0.0 copy-start.1
  7.7 0.0 copy-start.2
  7.7 0.0 copy-start.3
  7.7 0.0 copy-start.6
  7.7 0.0 copy-start.8
  7.7 3.8 %shard_map.132 = (f32[2,256,512]{2,1,0:T(8,128)S(1)}, bf16[2,256,512]{2,1,0:T(8,128)(2,1)S(1)}, bf16[2,256,512]{2,1,0:T(8,128)(2,1)S(1)}, bf16[256,512]{1,0:T(8,...) custom-call(bf16[400,512]{1,0:T(8,128)(2,1)S(1)} %collective-permute-done.1.near, s32[6,256]{1,0:T(8,128)} %links.1, ...), custom_call_target="tpu_custom_call" | custom-call | tf_op jit(solution)/shard_map/pallas_call | solution.py:353
  11.5 4.4 %collective-permute-done.far = bf16[400,512]{1,0:T(8,128)(2,1)S(1)} collective-permute-done((bf16[400,512]{1,0:T(8,128)(2,1)S(1)}, bf16[400,512]{1,0:T(8,128)(2,1)S(1)}, u32[]{:S(2)}, u32[]{:S(2)}) %collective-permute-start) | collective-permute-done | bytes 409632 | tf_op jit(solution)/shard_map/ppermute | solution.py:351
  15.9 0.0 copy-done
  15.9 0.0 copy-done.1
  15.9 0.0 copy-done.2
  15.9 0.0 copy-done.3
  15.9 0.0 copy-done.6
  15.9 0.0 copy-done.8
  15.9 0.0 copy-start.4
  15.9 0.0 copy-start.5
  16.0 0.0 copy-start.7
  16.0 3.6 %shard_map.133 = (f32[83,512]{1,0:T(8,128)S(1)}, bf16[83,512]{1,0:T(8,128)(2,1)S(1)}) custom-call(bf16[2,256,512]{2,1,0:T(8,128)(2,1)S(1)} %copy-done.1, s32[6,256]{1,0:T(8,128)S(1)} %copy-done.6, bf16[400,512]{1,0:T(8,128)(2,1)S(1)} %collective-permute-done.far, f32[2,2,512]{2,1,0:T(2,128)S(1)} %get-tuple-element.16.scaling, ...), custom_call_target="tpu_custom_call" | custom-call | tf_op jit(solution)/shard_map/pallas_call | solution.py:377
  19.6 10.6 %collective-permute-start.2 = (bf16[83,512]{1,0:T(8,128)(2,1)S(1)}, bf16[83,512]{1,0:T(8,128)(2,1)S(1)}, u32[]{:S(2)}, u32[]{:S(2)}) collective-permute-start(bf16[83,512]{1,0:T(8,128)(2,1)S(1)} %get-tuple-element.21.mine.rounded), channel_id=1, source_target_pairs={{0,64},{64,0},{128,192},{192,128},{256,320},{320,256},{384,448},{4... | collective-permute-start | bytes 254984 | tf_op jit(solution)/shard_map/ppermute | solution.py:391
  30.2 0.0 copy-done.4
  30.2 0.0 copy-done.5
  30.2 0.0 copy-done.7
  30.2 0.6 %shard_map.134.base = f32[2,83,1024]{2,1,0:T(8,128)S(1)} custom-call(f32[83,512]{1,0:T(8,128)S(1)} %get-tuple-element.22.decoded, bf16[83,1024]{1,0:T(8,128)(2,1)S(1)} %copy-done.4, bf16[83,1024]{1,0:T(8,128)(2,1)S(1)} %copy-done.5, f32[1,1024]{1,0:T(1,128)S(1)} %bitcast.3, bf16[256,1024]{1,0:T(8,128)(2,1)S(1)} %get-tuple-element.23.incidence), custom_call_target="tpu_custom_call" | custom-call | tf_op jit(solution)/shard_map/pallas_call | solution.py:393
  30.8 2.1 %collective-permute-done.2.partner = bf16[83,512]{1,0:T(8,128)(2,1)S(1)} collective-permute-done((bf16[83,512]{1,0:T(8,128)(2,1)S(1)}, bf16[83,512]{1,0:T(8,128)(2,1)S(1)}, u32[]{:S(2)}, u32[]{:S(2)}) %collective-permute-start.2) | collective-permute-done | bytes 85024 | tf_op jit(solution)/shard_map/ppermute | solution.py:391
  32.9 0.1 shard_map.135
  32.9 15.0 %all_to_all.5.others = bf16[4,83,1024]{2,1,0:T(8,128)(2,1)S(1)} all-to-all(bf16[4,83,1024]{2,1,0:T(8,128)(2,1)S(1)} %shard_map.135), channel_id=1, replica_groups={{0,128,256,384},{64,192,320,448},{1,129,257,385},{65,193,321,449},{2,13..., dimensions={0} | all-to-all | bytes 1359872 | tf_op jit(solution)/shard_map/all_to_all | solution.py:401
  47.9 3.6 %shard_map.136 = (bf16[2,83,1024]{2,1,0:T(8,128)(2,1)S(1)}, bf16[2,256,512]{2,1,0:T(8,128)(2,1)}) custom-call(bf16[83,512]{1,0:T(8,128)(2,1)S(1)} %get-tuple-element.21.mine.rounded, bf16[4,83,1024]{2,1,0:T(8,128)(2,1)S(1)} %all_to_all.5.others, bf16[256,1024]{1,0:T(8,128)(2,1)S(1)} %get-tuple-element.23.incidence, f32[2,83,1024]{2,1,0:T(8,128)S(1)} %shard_map.134.base, ...), custom_call_target="tpu_custom_call" | custom-call | tf_op jit(solution)/shard_map/pallas_call | solution.py:405
  51.5 1.1 %copy.14 = bf16[2,83,1024]{2,0,1:T(2,128)(2,1)} copy(bf16[2,83,1024]{2,1,0:T(8,128)(2,1)S(1)} %get-tuple-element.26) | data formatting | bytes 679936 | tf_op jit(solution)/shard_map/pallas_call | solution.py:405
Async XLA Ops:
  1.9 5.7 %collective-permute-start.1 = (bf16[400,512]{1,0:T(8,128)(2,1)S(1)}, bf16[400,512]{1,0:T(8,128)(2,1)S(1)}, u32[]{:S(2)}, u32[]{:S(2)}) collective-permute-start(bf16[400,512]{1,0:T(8,128)(2,1)S(1)} %get-tuple-element.15), channel_id=1, source_target_pairs={{0,1},{1,0},{2,3},{3,2},{4,5},{5,4},{6,7},{7,6},{8,9},{9,8},{10,11... | collective-permute-start | bytes 1228808 | tf_op jit(solution)/shard_map/ppermute | solution.py:352
  4.5 11.4 %collective-permute-start = (bf16[400,512]{1,0:T(8,128)(2,1)S(1)}, bf16[400,512]{1,0:T(8,128)(2,1)S(1)}, u32[]{:S(2)}, u32[]{:S(2)}) collective-permute-start(bf16[400,512]{1,0:T(8,128)(2,1)S(1)} %get-tuple-element.14), channel_id=1, source_target_pairs={{0,63},{1,2},{2,1},{3,4},{4,3},{5,6},{6,5},{7,8},{8,7},{9,10},{10,... | collective-permute-start | bytes 1228808 | tf_op jit(solution)/shard_map/ppermute | solution.py:351
  7.6 8.3 %copy-start = (bf16[2,1024,512]{2,1,0:T(8,128)(2,1)S(1)}, bf16[2,1024,512]{2,1,0:T(8,128)(2,1)}, u32[]{:S(2)}) copy-start(bf16[2,1024,512]{2,1,0:T(8,128)(2,1)} %w_in.1) | copy-start | bytes 6291460
  7.6 8.3 %copy-start.1 = (bf16[2,256,512]{2,1,0:T(8,128)(2,1)S(1)}, bf16[2,256,512]{2,1,0:T(8,128)(2,1)}, u32[]{:S(2)}) copy-start(bf16[2,256,512]{2,1,0:T(8,128)(2,1)} %latent.3) | copy-start | bytes 1572868
  7.7 8.2 %copy-start.2 = (bf16[2,512,512]{2,1,0:T(8,128)(2,1)S(1)}, bf16[2,512,512]{2,1,0:T(8,128)(2,1)}, u32[]{:S(2)}) copy-start(bf16[2,512,512]{2,1,0:T(8,128)(2,1)} %w_out.1) | copy-start | bytes 3145732
  7.7 8.2 %copy-start.3 = (bf16[83,512]{1,0:T(8,128)(2,1)S(1)}, bf16[83,512]{1,0:T(8,128)(2,1)}, u32[]{:S(2)}) copy-start(bf16[83,512]{1,0:T(8,128)(2,1)} %w_dec.3) | copy-start | bytes 254980
  7.7 8.2 %copy-start.6 = (s32[6,256]{1,0:T(8,128)S(1)}, s32[6,256]{1,0:T(8,128)}, u32[]{:S(2)}) copy-start(s32[6,256]{1,0:T(8,128)} %links.1) | copy-start | bytes 18436
  7.7 8.2 %copy-start.8 = (f32[512]{0:T(512)S(1)}, f32[512]{0:T(512)}, u32[]{:S(2)}) copy-start(f32[512]{0:T(512)} %param.18) | copy-start | bytes 6148
  15.9 14.3 %copy-start.4 = (bf16[83,1024]{1,0:T(8,128)(2,1)S(1)}, bf16[83,1024]{1,0:T(8,128)(2,1)}, u32[]{:S(2)}) copy-start(bf16[83,1024]{1,0:T(8,128)(2,1)} %prior.1) | copy-start | bytes 509956
  15.9 14.3 %copy-start.5 = (bf16[83,1024]{1,0:T(8,128)(2,1)S(1)}, bf16[83,1024]{1,0:T(8,128)(2,1)}, u32[]{:S(2)}) copy-start(bf16[83,1024]{1,0:T(8,128)(2,1)} %target.1) | copy-start | bytes 509956
  16.0 14.3 %copy-start.7 = (f32[1024]{0:T(1024)S(1)}, f32[1024]{0:T(1024)}, u32[]{:S(2)}) copy-start(f32[1024]{0:T(1024)} %param.23) | copy-start | bytes 12292
  19.6 13.3 %collective-permute-start.2 = (bf16[83,512]{1,0:T(8,128)(2,1)S(1)}, bf16[83,512]{1,0:T(8,128)(2,1)S(1)}, u32[]{:S(2)}, u32[]{:S(2)}) collective-permute-start(bf16[83,512]{1,0:T(8,128)(2,1)S(1)} %get-tuple-element.21.mine.rounded), channel_id=1, source_target_pairs={{0,64},{64,0},{128,192},{192,128},{256,320},{320,256},{384,448},{4... | collective-permute-start | bytes 254984 | tf_op jit(solution)/shard_map/ppermute | solution.py:391

commit v4 on v3

--- a/solution.py
+++ b/solution.py
@@ -291,7 +291,7 @@
 
 
 def score_kernel(
-    ensemble, rounded, others, incidence, base, weight, w_dec, grad_out, vertex_out, grads, vertices, sems
+    ensemble, rounded, others, incidence, base, weight, w_dec, grad_out, vertex_out, grads, both, vertices, sems
 ):
     members, channels, _ = base.shape
     nodes = incidence.shape[0]
@@ -302,12 +302,13 @@
     for member in range(members):
         high, low = at_points[2 * member : 2 * member + 2]
         grads[member] = (base[member] - factor * (low + high)).astype(BF)
-        copies.append(pltpu.make_async_copy(grads.at[member], grad_out.at[member], sems.at[0, member]))
-        copies[-1].start()
+    both[...] = jnp.stack([grads[member] for member in range(members)], axis=1)
+    copies.append(pltpu.make_async_copy(both, grad_out, sems.at[members]))
+    copies[-1].start()
     for member in range(members):
         high, middle, low = parts_of(dot_nt(incidence[...], grads[member]), 3)
         vertices[member] = (dot(low, w_dec[...]) + dot(middle, w_dec[...]) + dot(high, w_dec[...])).astype(BF)
-        copies.append(pltpu.make_async_copy(vertices.at[member], vertex_out.at[member], sems.at[1, member]))
+        copies.append(pltpu.make_async_copy(vertices.at[member], vertex_out.at[member], sems.at[member]))
         copies[-1].start()
     for copy in copies:
         copy.wait()
@@ -402,13 +403,19 @@
         stacked, "member", split_axis=0, concat_axis=0, tiled=True,
         axis_index_groups=[list(range(side, groups, sides)) for side in range(sides)],
     )
-    return call(
+    grads, vertices = call(
         functools.partial(score_kernel, ensemble),
-        [((members, channels, points), BF), ((members, rows, depth), BF)],
+        [((channels, members, points), BF), ((members, rows, depth), BF)],
         [VMEM] * 6,
-        [((members, channels, points), BF), ((members, rows, depth), BF), dma((2, members))],
+        [
+            ((members, channels, points), BF),
+            ((channels, members, points), BF),
+            ((members, rows, depth), BF),
+            dma((members + 1,)),
+        ],
         HBM,
     )(rounded, others, incidence, base, weight, w_dec)
+    return jnp.transpose(grads, (1, 0, 2)), vertices
 
 
 def solution(mesh):

time: 52.8 us -> 51.6 us (0.977)
  local copies, waits for them, and re-layouts: 1.14 us -> 0.06 us
    pallas_call x1 -> x0, local copies, waits for them, and re-layouts: 1.08 us -> none  [per_device(): call(functools.partial(score_kernel, ensemble), [((members, channels, poi...]
where the time goes in v4:
time: 51.6 us; the launch traced here: 51.4 us
  starting transfers between devices  16.3 us (32%)
  blocking collectives  14.9 us (29%)
  Pallas kernels  12.8 us (25%)
  waiting for transfers between devices  6.46 us (13%)
  between operations  0.82 us (2%)
    all_to_all x1, blocking collectives, per_device(): lax.all_to_all(stacked, 'member', split_axis=0, concat_axis=0, tiled=True...  14.9 us
    ppermute x1, starting transfers between devices, per_device(): lax.ppermute(rounded, 'member', [(i, i ^ 1) for i in range(groups)])  10.6 us
    ppermute x1, waiting for transfers between devices, per_device(): far = lax.ppermute(far, 'node', far_pairs)  4.38 us
    pallas_call x1, Pallas kernels, per_device(): call(functools.partial(near_kernel, shards), [((members, rows, depth), F3...  3.8 us
    pallas_call x1, Pallas kernels, per_device(): call(functools.partial(far_kernel, shards), [((channels, members * rows),...  3.6 us
    pallas_call x1, Pallas kernels, per_device(): call(functools.partial(score_kernel, ensemble), [((channels, members, poi...  3.51 us
    ppermute x1, starting transfers between devices, per_device(): far = lax.ppermute(far, 'node', far_pairs)  3.1 us
    ppermute x1, starting transfers between devices, per_device(): near = lax.ppermute(near, 'node', near_pairs)  2.58 us
  transfers between devices with their start and end apart: 3, of which 2 were waited for; matrix products, arithmetic and copies ran while one was open for 0% of the time, Pallas kernels for 8%

profile of v4, /device:TPU:57, one launch (start us, length us, event | category | flops | bytes accessed | tf_op | source)
XLA Modules:
  0.0 51.4 jit_solution(7331726619600382678)
XLA Ops:
  0.6 1.3 %shard_map.131 = (bf16[400,512]{1,0:T(8,128)(2,1)S(1)}, bf16[400,512]{1,0:T(8,128)(2,1)S(1)}) custom-call(bf16[2,256,512]{2,1,0:T(8,128)(2,1)} %latent.3, s32[6,256]{1,0:T(8,128)} %links.1), custom_call_target="tpu_custom_call" | custom-call | tf_op jit(solution)/shard_map/pallas_call | solution.py:349
  1.9 2.6 %collective-permute-start.1 = (bf16[400,512]{1,0:T(8,128)(2,1)S(1)}, bf16[400,512]{1,0:T(8,128)(2,1)S(1)}, u32[]{:S(2)}, u32[]{:S(2)}) collective-permute-start(bf16[400,512]{1,0:T(8,128)(2,1)S(1)} %get-tuple-element.17), channel_id=1, source_target_pairs={{0,1},{1,0},{2,3},{3,2},{4,5},{5,4},{6,7},{7,6},{8,9},{9,8},{10,11... | collective-permute-start | bytes 1228808 | tf_op jit(solution)/shard_map/ppermute | solution.py:353
  4.5 3.1 %collective-permute-start = (bf16[400,512]{1,0:T(8,128)(2,1)S(1)}, bf16[400,512]{1,0:T(8,128)(2,1)S(1)}, u32[]{:S(2)}, u32[]{:S(2)}) collective-permute-start(bf16[400,512]{1,0:T(8,128)(2,1)S(1)} %get-tuple-element.16), channel_id=1, source_target_pairs={{0,63},{1,2},{2,1},{3,4},{4,3},{5,6},{6,5},{7,8},{8,7},{9,10},{10,... | collective-permute-start | bytes 1228808 | tf_op jit(solution)/shard_map/ppermute | solution.py:352
  7.6 0.0 collective-permute-done.1.near
  7.6 0.0 copy-start
  7.6 0.0 copy-start.1
  7.7 0.0 copy-start.2
  7.7 0.0 copy-start.3
  7.7 0.0 copy-start.6
  7.7 0.0 copy-start.8
  7.7 3.8 %shard_map.132 = (f32[2,256,512]{2,1,0:T(8,128)S(1)}, bf16[2,256,512]{2,1,0:T(8,128)(2,1)S(1)}, bf16[2,256,512]{2,1,0:T(8,128)(2,1)S(1)}, bf16[256,512]{1,0:T(8,...) custom-call(bf16[400,512]{1,0:T(8,128)(2,1)S(1)} %collective-permute-done.1.near, s32[6,256]{1,0:T(8,128)} %links.1, ...), custom_call_target="tpu_custom_call" | custom-call | tf_op jit(solution)/shard_map/pallas_call | solution.py:354
  11.5 4.4 %collective-permute-done.far = bf16[400,512]{1,0:T(8,128)(2,1)S(1)} collective-permute-done((bf16[400,512]{1,0:T(8,128)(2,1)S(1)}, bf16[400,512]{1,0:T(8,128)(2,1)S(1)}, u32[]{:S(2)}, u32[]{:S(2)}) %collective-permute-start) | collective-permute-done | bytes 409632 | tf_op jit(solution)/shard_map/ppermute | solution.py:352
  15.9 0.0 copy-done
  15.9 0.0 copy-done.1
  15.9 0.0 copy-done.2
  15.9 0.0 copy-done.3
  15.9 0.0 copy-done.6
  15.9 0.0 copy-done.8
  15.9 0.0 copy-start.4
  15.9 0.0 copy-start.5
  16.0 0.0 copy-start.7
  16.0 3.6 %shard_map.133 = (f32[83,512]{1,0:T(8,128)S(1)}, bf16[83,512]{1,0:T(8,128)(2,1)S(1)}) custom-call(bf16[2,256,512]{2,1,0:T(8,128)(2,1)S(1)} %copy-done.1, s32[6,256]{1,0:T(8,128)S(1)} %copy-done.6, bf16[400,512]{1,0:T(8,128)(2,1)S(1)} %collective-permute-done.far, f32[2,2,512]{2,1,0:T(2,128)S(1)} %get-tuple-element.18.scaling, ...), custom_call_target="tpu_custom_call" | custom-call | tf_op jit(solution)/shard_map/pallas_call | solution.py:378
  19.6 10.6 %collective-permute-start.2 = (bf16[83,512]{1,0:T(8,128)(2,1)S(1)}, bf16[83,512]{1,0:T(8,128)(2,1)S(1)}, u32[]{:S(2)}, u32[]{:S(2)}) collective-permute-start(bf16[83,512]{1,0:T(8,128)(2,1)S(1)} %get-tuple-element.23.mine.rounded), channel_id=1, source_target_pairs={{0,64},{64,0},{128,192},{192,128},{256,320},{320,256},{384,448},{4... | collective-permute-start | bytes 254984 | tf_op jit(solution)/shard_map/ppermute | solution.py:392
  30.2 0.0 copy-done.4
  30.2 0.0 copy-done.5
  30.2 0.0 copy-done.7
  30.2 0.6 %shard_map.134.base = f32[2,83,1024]{2,1,0:T(8,128)S(1)} custom-call(f32[83,512]{1,0:T(8,128)S(1)} %get-tuple-element.24.decoded, bf16[83,1024]{1,0:T(8,128)(2,1)S(1)} %copy-done.4, bf16[83,1024]{1,0:T(8,128)(2,1)S(1)} %copy-done.5, f32[1,1024]{1,0:T(1,128)S(1)} %bitcast.4, bf16[256,1024]{1,0:T(8,128)(2,1)S(1)} %get-tuple-element.25.incidence), custom_call_target="tpu_custom_call" | custom-call | tf_op jit(solution)/shard_map/pallas_call | solution.py:394
  30.8 2.1 %collective-permute-done.2.partner = bf16[83,512]{1,0:T(8,128)(2,1)S(1)} collective-permute-done((bf16[83,512]{1,0:T(8,128)(2,1)S(1)}, bf16[83,512]{1,0:T(8,128)(2,1)S(1)}, u32[]{:S(2)}, u32[]{:S(2)}) %collective-permute-start.2) | collective-permute-done | bytes 85024 | tf_op jit(solution)/shard_map/ppermute | solution.py:392
  32.9 0.1 shard_map.135
  32.9 14.9 %all_to_all.5.others = bf16[4,83,1024]{2,1,0:T(8,128)(2,1)S(1)} all-to-all(bf16[4,83,1024]{2,1,0:T(8,128)(2,1)S(1)} %shard_map.135), channel_id=1, replica_groups={{0,128,256,384},{64,192,320,448},{1,129,257,385},{65,193,321,449},{2,13..., dimensions={0} | all-to-all | bytes 1359872 | tf_op jit(solution)/shard_map/all_to_all | solution.py:402
  47.9 3.5 %shard_map.136 = (bf16[83,2,1024]{2,1,0:T(2,128)(2,1)}, bf16[2,256,512]{2,1,0:T(8,128)(2,1)}) custom-call(bf16[83,512]{1,0:T(8,128)(2,1)S(1)} %get-tuple-element.23.mine.rounded, bf16[4,83,1024]{2,1,0:T(8,128)(2,1)S(1)} %all_to_all.5.others, bf16[256,1024]{1,0:T(8,128)(2,1)S(1)} %get-tuple-element.25.incidence, f32[2,83,1024]{2,1,0:T(8,128)S(1)} %shard_map.134.base, ...), custom_call_target="tpu_custom_call" | custom-call | tf_op jit(solution)/shard_map/pallas_call | solution.py:406
Async XLA Ops:
  1.9 5.7 %collective-permute-start.1 = (bf16[400,512]{1,0:T(8,128)(2,1)S(1)}, bf16[400,512]{1,0:T(8,128)(2,1)S(1)}, u32[]{:S(2)}, u32[]{:S(2)}) collective-permute-start(bf16[400,512]{1,0:T(8,128)(2,1)S(1)} %get-tuple-element.17), channel_id=1, source_target_pairs={{0,1},{1,0},{2,3},{3,2},{4,5},{5,4},{6,7},{7,6},{8,9},{9,8},{10,11... | collective-permute-start | bytes 1228808 | tf_op jit(solution)/shard_map/ppermute | solution.py:353
  4.5 11.4 %collective-permute-start = (bf16[400,512]{1,0:T(8,128)(2,1)S(1)}, bf16[400,512]{1,0:T(8,128)(2,1)S(1)}, u32[]{:S(2)}, u32[]{:S(2)}) collective-permute-start(bf16[400,512]{1,0:T(8,128)(2,1)S(1)} %get-tuple-element.16), channel_id=1, source_target_pairs={{0,63},{1,2},{2,1},{3,4},{4,3},{5,6},{6,5},{7,8},{8,7},{9,10},{10,... | collective-permute-start | bytes 1228808 | tf_op jit(solution)/shard_map/ppermute | solution.py:352
  7.6 8.3 %copy-start = (bf16[2,1024,512]{2,1,0:T(8,128)(2,1)S(1)}, bf16[2,1024,512]{2,1,0:T(8,128)(2,1)}, u32[]{:S(2)}) copy-start(bf16[2,1024,512]{2,1,0:T(8,128)(2,1)} %w_in.1) | copy-start | bytes 6291460
  7.6 8.3 %copy-start.1 = (bf16[2,256,512]{2,1,0:T(8,128)(2,1)S(1)}, bf16[2,256,512]{2,1,0:T(8,128)(2,1)}, u32[]{:S(2)}) copy-start(bf16[2,256,512]{2,1,0:T(8,128)(2,1)} %latent.3) | copy-start | bytes 1572868
  7.7 8.2 %copy-start.2 = (bf16[2,512,512]{2,1,0:T(8,128)(2,1)S(1)}, bf16[2,512,512]{2,1,0:T(8,128)(2,1)}, u32[]{:S(2)}) copy-start(bf16[2,512,512]{2,1,0:T(8,128)(2,1)} %w_out.1) | copy-start | bytes 3145732
  7.7 8.2 %copy-start.3 = (bf16[83,512]{1,0:T(8,128)(2,1)S(1)}, bf16[83,512]{1,0:T(8,128)(2,1)}, u32[]{:S(2)}) copy-start(bf16[83,512]{1,0:T(8,128)(2,1)} %w_dec.3) | copy-start | bytes 254980
  7.7 8.2 %copy-start.6 = (s32[6,256]{1,0:T(8,128)S(1)}, s32[6,256]{1,0:T(8,128)}, u32[]{:S(2)}) copy-start(s32[6,256]{1,0:T(8,128)} %links.1) | copy-start | bytes 18436
  7.7 8.2 %copy-start.8 = (f32[512]{0:T(512)S(1)}, f32[512]{0:T(512)}, u32[]{:S(2)}) copy-start(f32[512]{0:T(512)} %param.18) | copy-start | bytes 6148
  15.9 14.3 %copy-start.4 = (bf16[83,1024]{1,0:T(8,128)(2,1)S(1)}, bf16[83,1024]{1,0:T(8,128)(2,1)}, u32[]{:S(2)}) copy-start(bf16[83,1024]{1,0:T(8,128)(2,1)} %prior.1) | copy-start | bytes 509956
  15.9 14.3 %copy-start.5 = (bf16[83,1024]{1,0:T(8,128)(2,1)S(1)}, bf16[83,1024]{1,0:T(8,128)(2,1)}, u32[]{:S(2)}) copy-start(bf16[83,1024]{1,0:T(8,128)(2,1)} %target.1) | copy-start | bytes 509956
  16.0 14.3 %copy-start.7 = (f32[1024]{0:T(1024)S(1)}, f32[1024]{0:T(1024)}, u32[]{:S(2)}) copy-start(f32[1024]{0:T(1024)} %param.23) | copy-start | bytes 12292
  19.6 13.3 %collective-permute-start.2 = (bf16[83,512]{1,0:T(8,128)(2,1)S(1)}, bf16[83,512]{1,0:T(8,128)(2,1)S(1)}, u32[]{:S(2)}, u32[]{:S(2)}) collective-permute-start(bf16[83,512]{1,0:T(8,128)(2,1)S(1)} %get-tuple-element.23.mine.rounded), channel_id=1, source_target_pairs={{0,64},{64,0},{128,192},{192,128},{256,320},{320,256},{384,448},{4... | collective-permute-start | bytes 254984 | tf_op jit(solution)/shard_map/ppermute | solution.py:392

commit v5 on v4

--- a/solution.py
+++ b/solution.py
@@ -209,7 +209,6 @@
     far_at = pl.multiple_of(odd * rows, 64)
     near_at = pl.multiple_of(even * halo, 64)
     for member in range(members):
-        window[member, 2 * halo :] = jnp.zeros((window.shape[1] - 2 * halo, window.shape[2]), BF)
         window_next[member, filled:] = jnp.zeros((window_next.shape[1] - filled, window_next.shape[2]), BF)
         edge = far[member * halo : (member + 1) * halo]
         window[member, pl.ds(pl.multiple_of(odd * halo, 64), halo)] = norm(
@@ -295,19 +294,24 @@
 ):
     members, channels, _ = base.shape
     nodes = incidence.shape[0]
+    lanes = grads.shape[1]
     factor = weight[...] * (1.0 / (ensemble * (ensemble - 1)))
     copies = []
     pull = [part for m in range(members) for part in parts_of(pull_sums(rounded, others, m, members), 2)]
     at_points = at_grid(pull, incidence)
     for member in range(members):
         high, low = at_points[2 * member : 2 * member + 2]
-        grads[member] = (base[member] - factor * (low + high)).astype(BF)
-    both[...] = jnp.stack([grads[member] for member in range(members)], axis=1)
+        grad = (base[member] - factor * (low + high)).astype(BF)
+        grads[member] = jnp.concatenate([grad, jnp.zeros((lanes - channels, grad.shape[1]), BF)], axis=0)
+    both[...] = jnp.stack([grads[member, :channels] for member in range(members)], axis=1)
     copies.append(pltpu.make_async_copy(both, grad_out, sems.at[members]))
     copies[-1].start()
-    for member in range(members):
-        high, middle, low = parts_of(dot_nt(incidence[...], grads[member]), 3)
-        vertices[member] = (dot(low, w_dec[...]) + dot(middle, w_dec[...]) + dot(high, w_dec[...])).astype(BF)
+    by_node = dot_nt(incidence[...], jnp.concatenate([grads[member] for member in range(members)], axis=0))
+    filled = jnp.concatenate([w_dec[...], jnp.zeros((lanes - channels, w_dec.shape[1]), BF)], axis=0)
+    weights = jnp.concatenate([filled, filled], axis=0)
+    for member in range(members):
+        parts = parts_of(by_node[:, member * lanes : (member + 1) * lanes], 2)
+        vertices[member] = dot(jnp.concatenate(parts, axis=1), weights).astype(BF)
         copies.append(pltpu.make_async_copy(vertices.at[member], vertex_out.at[member], sems.at[member]))
         copies[-1].start()
     for copy in copies:
@@ -380,7 +384,7 @@
         [((channels, members * rows), F32), ((channels, members * rows), BF)],
         [VMEM] * 12,
         [
-            ((members, padded(2 * halo), depth), BF),
+            ((members, 2 * halo, depth), BF),
             ((members, halo, depth), BF),
             ((members, rows + halo, depth), F32),
             ((members, wide, depth), BF),
@@ -408,7 +412,7 @@
         [((channels, members, points), BF), ((members, rows, depth), BF)],
         [VMEM] * 6,
         [
-            ((members, channels, points), BF),
+            ((members, channels + -channels % 128, points), BF),
             ((channels, members, points), BF),
             ((members, rows, depth), BF),
             dma((members + 1,)),

time: 51.6 us -> 51 us (0.988)
  Pallas kernels: 12.8 us -> 12.2 us
    pallas_call x1, Pallas kernels: 3.51 us -> 2.92 us  [per_device(): call(functools.partial(score_kernel, ensemble), [((channels, members, poi...]
  transfers between devices with their start and end apart: 3 -> 3, of which waited for: 2 -> 2; matrix products, arithmetic and copies ran while one was open for 0% -> 0% of each run, Pallas kernels for 8% -> 9%
where the time goes in v5:
time: 51 us; the launch traced here: 50.8 us
  starting transfers between devices  16.3 us (32%)
  blocking collectives  14.9 us (29%)
  Pallas kernels  12.2 us (24%)
  waiting for transfers between devices  6.46 us (13%)
  between operations  0.82 us (2%)
    all_to_all x1, blocking collectives, per_device(): lax.all_to_all(stacked, 'member', split_axis=0, concat_axis=0, tiled=True...  14.9 us
    ppermute x1, starting transfers between devices, per_device(): lax.ppermute(rounded, 'member', [(i, i ^ 1) for i in range(groups)])  10.6 us
    ppermute x1, waiting for transfers between devices, per_device(): far = lax.ppermute(far, 'node', far_pairs)  4.38 us
    pallas_call x1, Pallas kernels, per_device(): call(functools.partial(near_kernel, shards), [((members, rows, depth), F3...  3.8 us
    pallas_call x1, Pallas kernels, per_device(): call(functools.partial(far_kernel, shards), [((channels, members * rows),...  3.59 us
    ppermute x1, starting transfers between devices, per_device(): far = lax.ppermute(far, 'node', far_pairs)  3.1 us
    pallas_call x1, Pallas kernels, per_device(): call(functools.partial(score_kernel, ensemble), [((channels, members, poi...  2.92 us
    ppermute x1, starting transfers between devices, per_device(): near = lax.ppermute(near, 'node', near_pairs)  2.58 us
  transfers between devices with their start and end apart: 3, of which 2 were waited for; matrix products, arithmetic and copies ran while one was open for 0% of the time, Pallas kernels for 9%

profile of v5, /device:TPU:57, one launch (start us, length us, event | category | flops | bytes accessed | tf_op | source)
XLA Modules:
  0.0 50.8 jit_solution(4272025107920018939)
XLA Ops:
  0.6 1.3 %shard_map.131 = (bf16[400,512]{1,0:T(8,128)(2,1)S(1)}, bf16[400,512]{1,0:T(8,128)(2,1)S(1)}) custom-call(bf16[2,256,512]{2,1,0:T(8,128)(2,1)} %latent.3, s32[6,256]{1,0:T(8,128)} %links.1), custom_call_target="tpu_custom_call" | custom-call | tf_op jit(solution)/shard_map/pallas_call | solution.py:353
  1.9 2.6 %collective-permute-start.1 = (bf16[400,512]{1,0:T(8,128)(2,1)S(1)}, bf16[400,512]{1,0:T(8,128)(2,1)S(1)}, u32[]{:S(2)}, u32[]{:S(2)}) collective-permute-start(bf16[400,512]{1,0:T(8,128)(2,1)S(1)} %get-tuple-element.17), channel_id=1, source_target_pairs={{0,1},{1,0},{2,3},{3,2},{4,5},{5,4},{6,7},{7,6},{8,9},{9,8},{10,11... | collective-permute-start | bytes 1228808 | tf_op jit(solution)/shard_map/ppermute | solution.py:357
  4.5 3.1 %collective-permute-start = (bf16[400,512]{1,0:T(8,128)(2,1)S(1)}, bf16[400,512]{1,0:T(8,128)(2,1)S(1)}, u32[]{:S(2)}, u32[]{:S(2)}) collective-permute-start(bf16[400,512]{1,0:T(8,128)(2,1)S(1)} %get-tuple-element.16), channel_id=1, source_target_pairs={{0,63},{1,2},{2,1},{3,4},{4,3},{5,6},{6,5},{7,8},{8,7},{9,10},{10,... | collective-permute-start | bytes 1228808 | tf_op jit(solution)/shard_map/ppermute | solution.py:356
  7.6 0.0 collective-permute-done.1.near
  7.6 0.0 copy-start
  7.6 0.0 copy-start.1
  7.7 0.0 copy-start.2
  7.7 0.0 copy-start.3
  7.7 0.0 copy-start.6
  7.7 0.0 copy-start.8
  7.7 3.8 %shard_map.132 = (f32[2,256,512]{2,1,0:T(8,128)S(1)}, bf16[2,256,512]{2,1,0:T(8,128)(2,1)S(1)}, bf16[2,256,512]{2,1,0:T(8,128)(2,1)S(1)}, bf16[256,512]{1,0:T(8,...) custom-call(bf16[400,512]{1,0:T(8,128)(2,1)S(1)} %collective-permute-done.1.near, s32[6,256]{1,0:T(8,128)} %links.1, ...), custom_call_target="tpu_custom_call" | custom-call | tf_op jit(solution)/shard_map/pallas_call | solution.py:358
  11.5 4.4 %collective-permute-done.far = bf16[400,512]{1,0:T(8,128)(2,1)S(1)} collective-permute-done((bf16[400,512]{1,0:T(8,128)(2,1)S(1)}, bf16[400,512]{1,0:T(8,128)(2,1)S(1)}, u32[]{:S(2)}, u32[]{:S(2)}) %collective-permute-start) | collective-permute-done | bytes 409632 | tf_op jit(solution)/shard_map/ppermute | solution.py:356
  15.9 0.0 copy-done
  15.9 0.0 copy-done.1
  15.9 0.0 copy-done.2
  15.9 0.0 copy-done.3
  15.9 0.0 copy-done.6
  15.9 0.0 copy-done.8
  15.9 0.0 copy-start.4
  15.9 0.0 copy-start.5
  16.0 0.0 copy-start.7
  16.0 3.6 %shard_map.133 = (f32[83,512]{1,0:T(8,128)S(1)}, bf16[83,512]{1,0:T(8,128)(2,1)S(1)}) custom-call(bf16[2,256,512]{2,1,0:T(8,128)(2,1)S(1)} %copy-done.1, s32[6,256]{1,0:T(8,128)S(1)} %copy-done.6, bf16[400,512]{1,0:T(8,128)(2,1)S(1)} %collective-permute-done.far, f32[2,2,512]{2,1,0:T(2,128)S(1)} %get-tuple-element.18.scaling, ...), custom_call_target="tpu_custom_call" | custom-call | tf_op jit(solution)/shard_map/pallas_call | solution.py:382
  19.6 10.6 %collective-permute-start.2 = (bf16[83,512]{1,0:T(8,128)(2,1)S(1)}, bf16[83,512]{1,0:T(8,128)(2,1)S(1)}, u32[]{:S(2)}, u32[]{:S(2)}) collective-permute-start(bf16[83,512]{1,0:T(8,128)(2,1)S(1)} %get-tuple-element.23.mine.rounded), channel_id=1, source_target_pairs={{0,64},{64,0},{128,192},{192,128},{256,320},{320,256},{384,448},{4... | collective-permute-start | bytes 254984 | tf_op jit(solution)/shard_map/ppermute | solution.py:396
  30.2 0.0 copy-done.4
  30.2 0.0 copy-done.5
  30.2 0.0 copy-done.7
  30.2 0.6 %shard_map.134.base = f32[2,83,1024]{2,1,0:T(8,128)S(1)} custom-call(f32[83,512]{1,0:T(8,128)S(1)} %get-tuple-element.24.decoded, bf16[83,1024]{1,0:T(8,128)(2,1)S(1)} %copy-done.4, bf16[83,1024]{1,0:T(8,128)(2,1)S(1)} %copy-done.5, f32[1,1024]{1,0:T(1,128)S(1)} %bitcast.4, bf16[256,1024]{1,0:T(8,128)(2,1)S(1)} %get-tuple-element.25.incidence), custom_call_target="tpu_custom_call" | custom-call | tf_op jit(solution)/shard_map/pallas_call | solution.py:398
  30.8 2.1 %collective-permute-done.2.partner = bf16[83,512]{1,0:T(8,128)(2,1)S(1)} collective-permute-done((bf16[83,512]{1,0:T(8,128)(2,1)S(1)}, bf16[83,512]{1,0:T(8,128)(2,1)S(1)}, u32[]{:S(2)}, u32[]{:S(2)}) %collective-permute-start.2) | collective-permute-done | bytes 85024 | tf_op jit(solution)/shard_map/ppermute | solution.py:396
  32.9 0.1 shard_map.135
  32.9 14.9 %all_to_all.5.others = bf16[4,83,1024]{2,1,0:T(8,128)(2,1)S(1)} all-to-all(bf16[4,83,1024]{2,1,0:T(8,128)(2,1)S(1)} %shard_map.135), channel_id=1, replica_groups={{0,128,256,384},{64,192,320,448},{1,129,257,385},{65,193,321,449},{2,13..., dimensions={0} | all-to-all | bytes 1359872 | tf_op jit(solution)/shard_map/all_to_all | solution.py:406
  47.9 2.9 %shard_map.136 = (bf16[83,2,1024]{2,1,0:T(2,128)(2,1)}, bf16[2,256,512]{2,1,0:T(8,128)(2,1)}) custom-call(bf16[83,512]{1,0:T(8,128)(2,1)S(1)} %get-tuple-element.23.mine.rounded, bf16[4,83,1024]{2,1,0:T(8,128)(2,1)S(1)} %all_to_all.5.others, bf16[256,1024]{1,0:T(8,128)(2,1)S(1)} %get-tuple-element.25.incidence, f32[2,83,1024]{2,1,0:T(8,128)S(1)} %shard_map.134.base, ...), custom_call_target="tpu_custom_call" | custom-call | tf_op jit(solution)/shard_map/pallas_call | solution.py:410
Async XLA Ops:
  1.9 5.7 %collective-permute-start.1 = (bf16[400,512]{1,0:T(8,128)(2,1)S(1)}, bf16[400,512]{1,0:T(8,128)(2,1)S(1)}, u32[]{:S(2)}, u32[]{:S(2)}) collective-permute-start(bf16[400,512]{1,0:T(8,128)(2,1)S(1)} %get-tuple-element.17), channel_id=1, source_target_pairs={{0,1},{1,0},{2,3},{3,2},{4,5},{5,4},{6,7},{7,6},{8,9},{9,8},{10,11... | collective-permute-start | bytes 1228808 | tf_op jit(solution)/shard_map/ppermute | solution.py:357
  4.5 11.4 %collective-permute-start = (bf16[400,512]{1,0:T(8,128)(2,1)S(1)}, bf16[400,512]{1,0:T(8,128)(2,1)S(1)}, u32[]{:S(2)}, u32[]{:S(2)}) collective-permute-start(bf16[400,512]{1,0:T(8,128)(2,1)S(1)} %get-tuple-element.16), channel_id=1, source_target_pairs={{0,63},{1,2},{2,1},{3,4},{4,3},{5,6},{6,5},{7,8},{8,7},{9,10},{10,... | collective-permute-start | bytes 1228808 | tf_op jit(solution)/shard_map/ppermute | solution.py:356
  7.6 8.3 %copy-start = (bf16[2,1024,512]{2,1,0:T(8,128)(2,1)S(1)}, bf16[2,1024,512]{2,1,0:T(8,128)(2,1)}, u32[]{:S(2)}) copy-start(bf16[2,1024,512]{2,1,0:T(8,128)(2,1)} %w_in.1) | copy-start | bytes 6291460
  7.6 8.3 %copy-start.1 = (bf16[2,256,512]{2,1,0:T(8,128)(2,1)S(1)}, bf16[2,256,512]{2,1,0:T(8,128)(2,1)}, u32[]{:S(2)}) copy-start(bf16[2,256,512]{2,1,0:T(8,128)(2,1)} %latent.3) | copy-start | bytes 1572868
  7.7 8.2 %copy-start.2 = (bf16[2,512,512]{2,1,0:T(8,128)(2,1)S(1)}, bf16[2,512,512]{2,1,0:T(8,128)(2,1)}, u32[]{:S(2)}) copy-start(bf16[2,512,512]{2,1,0:T(8,128)(2,1)} %w_out.1) | copy-start | bytes 3145732
  7.7 8.2 %copy-start.3 = (bf16[83,512]{1,0:T(8,128)(2,1)S(1)}, bf16[83,512]{1,0:T(8,128)(2,1)}, u32[]{:S(2)}) copy-start(bf16[83,512]{1,0:T(8,128)(2,1)} %w_dec.3) | copy-start | bytes 254980
  7.7 8.2 %copy-start.6 = (s32[6,256]{1,0:T(8,128)S(1)}, s32[6,256]{1,0:T(8,128)}, u32[]{:S(2)}) copy-start(s32[6,256]{1,0:T(8,128)} %links.1) | copy-start | bytes 18436
  7.7 8.2 %copy-start.8 = (f32[512]{0:T(512)S(1)}, f32[512]{0:T(512)}, u32[]{:S(2)}) copy-start(f32[512]{0:T(512)} %param.18) | copy-start | bytes 6148
  15.9 14.3 %copy-start.4 = (bf16[83,1024]{1,0:T(8,128)(2,1)S(1)}, bf16[83,1024]{1,0:T(8,128)(2,1)}, u32[]{:S(2)}) copy-start(bf16[83,1024]{1,0:T(8,128)(2,1)} %prior.1) | copy-start | bytes 509956
  15.9 14.3 %copy-start.5 = (bf16[83,1024]{1,0:T(8,128)(2,1)S(1)}, bf16[83,1024]{1,0:T(8,128)(2,1)}, u32[]{:S(2)}) copy-start(bf16[83,1024]{1,0:T(8,128)(2,1)} %target.1) | copy-start | bytes 509956
  16.0 14.3 %copy-start.7 = (f32[1024]{0:T(1024)S(1)}, f32[1024]{0:T(1024)}, u32[]{:S(2)}) copy-start(f32[1024]{0:T(1024)} %param.23) | copy-start | bytes 12292
  19.6 13.3 %collective-permute-start.2 = (bf16[83,512]{1,0:T(8,128)(2,1)S(1)}, bf16[83,512]{1,0:T(8,128)(2,1)S(1)}, u32[]{:S(2)}, u32[]{:S(2)}) collective-permute-start(bf16[83,512]{1,0:T(8,128)(2,1)S(1)} %get-tuple-element.23.mine.rounded), channel_id=1, source_target_pairs={{0,64},{64,0},{128,192},{192,128},{256,320},{320,256},{384,448},{4... | collective-permute-start | bytes 254984 | tf_op jit(solution)/shard_map/ppermute | solution.py:396

commit v6 on v5

--- a/solution.py
+++ b/solution.py
@@ -80,8 +80,7 @@
     rows = values.shape[0] // len(windows)
     sums = [dot(counts, window)[:rows] for window in windows]
     neighbours = (jnp.concatenate(sums, axis=0) * (1.0 / link_count)).astype(BF)
-    depth = normed.shape[1]
-    preact = dot(normed, w_in[:depth]) + dot(neighbours, w_in[depth:])
+    preact = dot(jnp.concatenate([normed, neighbours], axis=1), w_in[...])
     return values + dot(silu(preact).astype(BF), w_out)
 
 
@@ -178,7 +177,7 @@
         fetch.wait()
     values = layer(
         rows_of(inputs, WIN, rows).astype(F32), rows_of(window, WIN, rows), [window[m] for m in range(members)],
-        counts, w_in[...], w_out[...], link_count,
+        counts, w_in, w_out[...], link_count,
     )
     for member in range(members):
         own = values[member * rows : (member + 1) * rows]
@@ -227,7 +226,7 @@
         window_next[member, pl.ds(near_at, rows)] = normed_next[member]
     values = layer(
         rows_of(inputs, 0, halo).astype(F32), rows_of(window, WIN, halo), [window[m] for m in range(members)],
-        counts, w_in[0], w_out[0], link_count,
+        counts, w_in.at[0], w_out[0], link_count,
     )
     for member in range(members):
         own = values[member * halo : (member + 1) * halo]
@@ -235,7 +234,7 @@
         window_next[member, pl.ds(far_at, halo)] = norm(own, scaling[1, member : member + 1])
     values = layer(
         rows_of(state, WIN, rows), rows_of(window_next, WIN, rows), [window_next[m] for m in range(members)],
-        counts_own[...], w_in[1], w_out[1], link_count,
+        counts_own[...], w_in.at[1], w_out[1], link_count,
     )
     decoded = dot_nt(w_dec[...], norm(values, dec_gain[...]))
     decoded_out[...] = decoded

time: 51 us -> 51.1 us (level)
  no operation moved by 1% of the time
where the time goes in v6:
time: 51.1 us; the launch traced here: 50.8 us
  starting transfers between devices  16.3 us (32%)
  blocking collectives  15 us (29%)
  Pallas kernels  12.2 us (24%)
  waiting for transfers between devices  6.46 us (13%)
  between operations  0.82 us (2%)
    all_to_all x1, blocking collectives, per_device(): lax.all_to_all(stacked, 'member', split_axis=0, concat_axis=0, tiled=True...  15 us
    ppermute x1, starting transfers between devices, per_device(): lax.ppermute(rounded, 'member', [(i, i ^ 1) for i in range(groups)])  10.6 us
    ppermute x1, waiting for transfers between devices, per_device(): far = lax.ppermute(far, 'node', far_pairs)  4.38 us
    pallas_call x1, Pallas kernels, per_device(): call(functools.partial(near_kernel, shards), [((members, rows, depth), F3...  3.8 us
    pallas_call x1, Pallas kernels, per_device(): call(functools.partial(far_kernel, shards), [((channels, members * rows),...  3.59 us
    ppermute x1, starting transfers between devices, per_device(): far = lax.ppermute(far, 'node', far_pairs)  3.1 us
    pallas_call x1, Pallas kernels, per_device(): call(functools.partial(score_kernel, ensemble), [((channels, members, poi...  2.92 us
    ppermute x1, starting transfers between devices, per_device(): near = lax.ppermute(near, 'node', near_pairs)  2.58 us
  transfers between devices with their start and end apart: 3, of which 2 were waited for; matrix products, arithmetic and copies ran while one was open for 0% of the time, Pallas kernels for 9%

profile of v6, /device:TPU:57, one launch (start us, length us, event | category | flops | bytes accessed | tf_op | source)
XLA Modules:
  0.0 50.8 jit_solution(17676855920736220734)
XLA Ops:
  0.6 1.3 %shard_map.131 = (bf16[400,512]{1,0:T(8,128)(2,1)S(1)}, bf16[400,512]{1,0:T(8,128)(2,1)S(1)}) custom-call(bf16[2,256,512]{2,1,0:T(8,128)(2,1)} %latent.3, s32[6,256]{1,0:T(8,128)} %links.1), custom_call_target="tpu_custom_call" | custom-call | tf_op jit(solution)/shard_map/pallas_call | solution.py:352
  1.9 2.6 %collective-permute-start.1 = (bf16[400,512]{1,0:T(8,128)(2,1)S(1)}, bf16[400,512]{1,0:T(8,128)(2,1)S(1)}, u32[]{:S(2)}, u32[]{:S(2)}) collective-permute-start(bf16[400,512]{1,0:T(8,128)(2,1)S(1)} %get-tuple-element.17), channel_id=1, source_target_pairs={{0,1},{1,0},{2,3},{3,2},{4,5},{5,4},{6,7},{7,6},{8,9},{9,8},{10,11... | collective-permute-start | bytes 1228808 | tf_op jit(solution)/shard_map/ppermute | solution.py:356
  4.5 3.1 %collective-permute-start = (bf16[400,512]{1,0:T(8,128)(2,1)S(1)}, bf16[400,512]{1,0:T(8,128)(2,1)S(1)}, u32[]{:S(2)}, u32[]{:S(2)}) collective-permute-start(bf16[400,512]{1,0:T(8,128)(2,1)S(1)} %get-tuple-element.16), channel_id=1, source_target_pairs={{0,63},{1,2},{2,1},{3,4},{4,3},{5,6},{6,5},{7,8},{8,7},{9,10},{10,... | collective-permute-start | bytes 1228808 | tf_op jit(solution)/shard_map/ppermute | solution.py:355
  7.6 0.0 collective-permute-done.1.near
  7.6 0.0 copy-start
  7.6 0.0 copy-start.1
  7.7 0.0 copy-start.2
  7.7 0.0 copy-start.3
  7.7 0.0 copy-start.6
  7.7 0.0 copy-start.8
  7.7 3.8 %shard_map.132 = (f32[2,256,512]{2,1,0:T(8,128)S(1)}, bf16[2,256,512]{2,1,0:T(8,128)(2,1)S(1)}, bf16[2,256,512]{2,1,0:T(8,128)(2,1)S(1)}, bf16[256,512]{1,0:T(8,...) custom-call(bf16[400,512]{1,0:T(8,128)(2,1)S(1)} %collective-permute-done.1.near, s32[6,256]{1,0:T(8,128)} %links.1, ...), custom_call_target="tpu_custom_call" | custom-call | tf_op jit(solution)/shard_map/pallas_call | solution.py:357
  11.5 4.4 %collective-permute-done.far = bf16[400,512]{1,0:T(8,128)(2,1)S(1)} collective-permute-done((bf16[400,512]{1,0:T(8,128)(2,1)S(1)}, bf16[400,512]{1,0:T(8,128)(2,1)S(1)}, u32[]{:S(2)}, u32[]{:S(2)}) %collective-permute-start) | collective-permute-done | bytes 409632 | tf_op jit(solution)/shard_map/ppermute | solution.py:355
  15.9 0.0 copy-done
  15.9 0.0 copy-done.1
  15.9 0.0 copy-done.2
  15.9 0.0 copy-done.3
  15.9 0.0 copy-done.6
  15.9 0.0 copy-done.8
  15.9 0.0 copy-start.4
  15.9 0.0 copy-start.5
  16.0 0.0 copy-start.7
  16.0 3.6 %shard_map.133 = (f32[83,512]{1,0:T(8,128)S(1)}, bf16[83,512]{1,0:T(8,128)(2,1)S(1)}) custom-call(bf16[2,256,512]{2,1,0:T(8,128)(2,1)S(1)} %copy-done.1, s32[6,256]{1,0:T(8,128)S(1)} %copy-done.6, bf16[400,512]{1,0:T(8,128)(2,1)S(1)} %collective-permute-done.far, f32[2,2,512]{2,1,0:T(2,128)S(1)} %get-tuple-element.18.scaling, ...), custom_call_target="tpu_custom_call" | custom-call | tf_op jit(solution)/shard_map/pallas_call | solution.py:381
  19.6 10.6 %collective-permute-start.2 = (bf16[83,512]{1,0:T(8,128)(2,1)S(1)}, bf16[83,512]{1,0:T(8,128)(2,1)S(1)}, u32[]{:S(2)}, u32[]{:S(2)}) collective-permute-start(bf16[83,512]{1,0:T(8,128)(2,1)S(1)} %get-tuple-element.23.mine.rounded), channel_id=1, source_target_pairs={{0,64},{64,0},{128,192},{192,128},{256,320},{320,256},{384,448},{4... | collective-permute-start | bytes 254984 | tf_op jit(solution)/shard_map/ppermute | solution.py:395
  30.2 0.0 copy-done.4
  30.2 0.0 copy-done.5
  30.2 0.0 copy-done.7
  30.2 0.6 %shard_map.134.base = f32[2,83,1024]{2,1,0:T(8,128)S(1)} custom-call(f32[83,512]{1,0:T(8,128)S(1)} %get-tuple-element.24.decoded, bf16[83,1024]{1,0:T(8,128)(2,1)S(1)} %copy-done.4, bf16[83,1024]{1,0:T(8,128)(2,1)S(1)} %copy-done.5, f32[1,1024]{1,0:T(1,128)S(1)} %bitcast.4, bf16[256,1024]{1,0:T(8,128)(2,1)S(1)} %get-tuple-element.25.incidence), custom_call_target="tpu_custom_call" | custom-call | tf_op jit(solution)/shard_map/pallas_call | solution.py:397
  30.8 2.1 %collective-permute-done.2.partner = bf16[83,512]{1,0:T(8,128)(2,1)S(1)} collective-permute-done((bf16[83,512]{1,0:T(8,128)(2,1)S(1)}, bf16[83,512]{1,0:T(8,128)(2,1)S(1)}, u32[]{:S(2)}, u32[]{:S(2)}) %collective-permute-start.2) | collective-permute-done | bytes 85024 | tf_op jit(solution)/shard_map/ppermute | solution.py:395
  32.9 0.1 shard_map.135
  32.9 15.0 %all_to_all.5.others = bf16[4,83,1024]{2,1,0:T(8,128)(2,1)S(1)} all-to-all(bf16[4,83,1024]{2,1,0:T(8,128)(2,1)S(1)} %shard_map.135), channel_id=1, replica_groups={{0,128,256,384},{64,192,320,448},{1,129,257,385},{65,193,321,449},{2,13..., dimensions={0} | all-to-all | bytes 1359872 | tf_op jit(solution)/shard_map/all_to_all | solution.py:405
  47.9 2.9 %shard_map.136 = (bf16[83,2,1024]{2,1,0:T(2,128)(2,1)}, bf16[2,256,512]{2,1,0:T(8,128)(2,1)}) custom-call(bf16[83,512]{1,0:T(8,128)(2,1)S(1)} %get-tuple-element.23.mine.rounded, bf16[4,83,1024]{2,1,0:T(8,128)(2,1)S(1)} %all_to_all.5.others, bf16[256,1024]{1,0:T(8,128)(2,1)S(1)} %get-tuple-element.25.incidence, f32[2,83,1024]{2,1,0:T(8,128)S(1)} %shard_map.134.base, ...), custom_call_target="tpu_custom_call" | custom-call | tf_op jit(solution)/shard_map/pallas_call | solution.py:409
Async XLA Ops:
  1.9 5.7 %collective-permute-start.1 = (bf16[400,512]{1,0:T(8,128)(2,1)S(1)}, bf16[400,512]{1,0:T(8,128)(2,1)S(1)}, u32[]{:S(2)}, u32[]{:S(2)}) collective-permute-start(bf16[400,512]{1,0:T(8,128)(2,1)S(1)} %get-tuple-element.17), channel_id=1, source_target_pairs={{0,1},{1,0},{2,3},{3,2},{4,5},{5,4},{6,7},{7,6},{8,9},{9,8},{10,11... | collective-permute-start | bytes 1228808 | tf_op jit(solution)/shard_map/ppermute | solution.py:356
  4.5 11.4 %collective-permute-start = (bf16[400,512]{1,0:T(8,128)(2,1)S(1)}, bf16[400,512]{1,0:T(8,128)(2,1)S(1)}, u32[]{:S(2)}, u32[]{:S(2)}) collective-permute-start(bf16[400,512]{1,0:T(8,128)(2,1)S(1)} %get-tuple-element.16), channel_id=1, source_target_pairs={{0,63},{1,2},{2,1},{3,4},{4,3},{5,6},{6,5},{7,8},{8,7},{9,10},{10,... | collective-permute-start | bytes 1228808 | tf_op jit(solution)/shard_map/ppermute | solution.py:355
  7.6 8.3 %copy-start = (bf16[2,1024,512]{2,1,0:T(8,128)(2,1)S(1)}, bf16[2,1024,512]{2,1,0:T(8,128)(2,1)}, u32[]{:S(2)}) copy-start(bf16[2,1024,512]{2,1,0:T(8,128)(2,1)} %w_in.1) | copy-start | bytes 6291460
  7.6 8.3 %copy-start.1 = (bf16[2,256,512]{2,1,0:T(8,128)(2,1)S(1)}, bf16[2,256,512]{2,1,0:T(8,128)(2,1)}, u32[]{:S(2)}) copy-start(bf16[2,256,512]{2,1,0:T(8,128)(2,1)} %latent.3) | copy-start | bytes 1572868
  7.7 8.2 %copy-start.2 = (bf16[2,512,512]{2,1,0:T(8,128)(2,1)S(1)}, bf16[2,512,512]{2,1,0:T(8,128)(2,1)}, u32[]{:S(2)}) copy-start(bf16[2,512,512]{2,1,0:T(8,128)(2,1)} %w_out.1) | copy-start | bytes 3145732
  7.7 8.2 %copy-start.3 = (bf16[83,512]{1,0:T(8,128)(2,1)S(1)}, bf16[83,512]{1,0:T(8,128)(2,1)}, u32[]{:S(2)}) copy-start(bf16[83,512]{1,0:T(8,128)(2,1)} %w_dec.3) | copy-start | bytes 254980
  7.7 8.2 %copy-start.6 = (s32[6,256]{1,0:T(8,128)S(1)}, s32[6,256]{1,0:T(8,128)}, u32[]{:S(2)}) copy-start(s32[6,256]{1,0:T(8,128)} %links.1) | copy-start | bytes 18436
  7.7 8.2 %copy-start.8 = (f32[512]{0:T(512)S(1)}, f32[512]{0:T(512)}, u32[]{:S(2)}) copy-start(f32[512]{0:T(512)} %param.18) | copy-start | bytes 6148
  15.9 14.3 %copy-start.4 = (bf16[83,1024]{1,0:T(8,128)(2,1)S(1)}, bf16[83,1024]{1,0:T(8,128)(2,1)}, u32[]{:S(2)}) copy-start(bf16[83,1024]{1,0:T(8,128)(2,1)} %prior.1) | copy-start | bytes 509956
  15.9 14.3 %copy-start.5 = (bf16[83,1024]{1,0:T(8,128)(2,1)S(1)}, bf16[83,1024]{1,0:T(8,128)(2,1)}, u32[]{:S(2)}) copy-start(bf16[83,1024]{1,0:T(8,128)(2,1)} %target.1) | copy-start | bytes 509956
  16.0 14.3 %copy-start.7 = (f32[1024]{0:T(1024)S(1)}, f32[1024]{0:T(1024)}, u32[]{:S(2)}) copy-start(f32[1024]{0:T(1024)} %param.23) | copy-start | bytes 12292
  19.6 13.3 %collective-permute-start.2 = (bf16[83,512]{1,0:T(8,128)(2,1)S(1)}, bf16[83,512]{1,0:T(8,128)(2,1)S(1)}, u32[]{:S(2)}, u32[]{:S(2)}) collective-permute-start(bf16[83,512]{1,0:T(8,128)(2,1)S(1)} %get-tuple-element.23.mine.rounded), channel_id=1, source_target_pairs={{0,64},{64,0},{128,192},{192,128},{256,320},{320,256},{384,448},{4... | collective-permute-start | bytes 254984 | tf_op jit(solution)/shard_map/ppermute | solution.py:395
